TPU v7x, 128 devices: a whole 4x4x4 slice. The times are simulated.
128 devices in a mesh: ctx: 32 (over z, x, core), head: 4 (over y).
Axes of the slice: x: 4, y: 4, z: 4, core: 2. Of those that a mesh axis runs over, the one named last changes fastest.
Arguments:
- q_raw: bfloat16 [16384, 32, 128], P('ctx', 'head'), may hold values from -12 to 12
- k_raw: bfloat16 [16384, 4, 128], P('ctx', 'head'), may hold values from -12 to 12
- values: bfloat16 [16384, 4, 128], P('ctx', 'head'), may hold values from -6 to 6
- dout: bfloat16 [16384, 32, 128], P('ctx', 'head'), may hold values from -6 to 6
- q_gain: float32 [128], replicated, may hold values from 1 to 6
- k_gain: float32 [128], replicated, may hold values from 1 to 6
- chosen: int32 [32, 4, 8], P('ctx', 'head'), may hold values from -1 to 30, as said below
Outputs:
- dq_raw: bfloat16 [16384, 32, 128], P('ctx', 'head')
- dk_raw: bfloat16 [16384, 4, 128], P('ctx', 'head')
- dvalues: bfloat16 [16384, 4, 128], P('ctx', 'head')
- q_gain_grad: float32 [128], replicated
- k_gain_grad: float32 [128], replicated
Inputs may be any that keep to these rules, and one draw needn't show every extreme that they name: chosen[b, g] lists min(8, b) different blocks below b, block b - 1 among them, and -1 in its other slots.
All inputs are finite; a program needn't handle non-finite values.
Results may differ from a plain program's by a relative error of at most 0.02.
The roundings to bfloat16 on the way count: a program that leaves them out, or rounds other values in their place, can miss the bound.
Values may be sent and summed in bfloat16 or wider, within the bound.
A program may use at most 128 MiB of HBM per device.

v0:
```python
import jax
import jax.numpy as jnp
from jax import lax
from jax.sharding import PartitionSpec as P

EPS = 1e-06


def norm_fwd(raw, gain):
    x = raw.astype(jnp.float32)
    scale_r = lax.rsqrt(jnp.mean(x * x, axis=-1, keepdims=True) + EPS)
    return (x, scale_r, (x * scale_r * gain).astype(jnp.bfloat16))


def norm_back(x, scale_r, gain, grad_y):
    along = gain * grad_y
    inner = jnp.mean(along * x, axis=-1, keepdims=True)
    grad_x = scale_r * (along - x * scale_r * scale_r * inner)
    return (grad_x, grad_y * x * scale_r)


def block_grads(q_grp, do_grp, keys, vals, valid):
    blk = q_grp.shape[1]
    slots = keys.shape[0] // blk
    scale = 1.0 / jnp.sqrt(jnp.float32(keys.shape[1]))
    rows = lax.broadcasted_iota(jnp.int32, (blk, blk), 0)
    cols = lax.broadcasted_iota(jnp.int32, (blk, blk), 1)
    chosen_mask = jnp.broadcast_to(jnp.repeat(valid, blk)[None, :], (blk, (slots - 1) * blk))
    mask = jnp.concatenate([chosen_mask, cols <= rows], axis=1)

    def one_head(carry, inputs):
        qh, doh = inputs
        scores = jnp.dot(qh, keys.T, preferred_element_type=jnp.float32) * scale
        scores = jnp.where(mask, scores, -jnp.inf)
        top = jnp.max(scores, axis=1, keepdims=True)
        expo = jnp.exp(scores - top)
        probs = expo / jnp.sum(expo, axis=1, keepdims=True)
        probs_b = probs.astype(jnp.bfloat16)
        attn_out = jnp.dot(probs_b, vals, preferred_element_type=jnp.float32)
        delta = jnp.sum(doh.astype(jnp.float32) * attn_out, axis=1, keepdims=True)
        dprobs = jnp.dot(doh, vals.T, preferred_element_type=jnp.float32)
        dscores = (probs * (dprobs - delta)).astype(jnp.bfloat16)
        dq = jnp.dot(dscores, keys, preferred_element_type=jnp.float32) * scale
        dk = carry[0] + jnp.dot(dscores.T, qh, preferred_element_type=jnp.float32) * scale
        dv = carry[1] + jnp.dot(probs_b.T, doh, preferred_element_type=jnp.float32)
        return ((dk, dv), dq)

    zeros = jnp.zeros(keys.shape, jnp.float32)
    (dk, dv), dq = lax.scan(one_head, (zeros, zeros), (q_grp, do_grp))
    return (dq, dk, dv)


def on_device(q_raw, k_raw, values, dout, q_gain, k_gain, chosen):
    blk, local_heads, width = q_raw.shape
    local_kv = k_raw.shape[1]
    topk = chosen.shape[2]
    position = lax.axis_index("ctx")
    xq, rq, qn = norm_fwd(q_raw, q_gain)
    xk, rk, kn = norm_fwd(k_raw, k_gain)
    idx = chosen[0]
    idxc = jnp.maximum(idx, 0)
    kv_range = jnp.arange(local_kv)[:, None]
    keys_all, vals_all = (
        lax.all_gather(kn, "ctx", axis=0, tiled=True),
        lax.all_gather(values, "ctx", axis=0, tiled=True),
    )
    nblocks = keys_all.shape[0] // blk
    key_blocks = keys_all.reshape(nblocks, blk, local_kv, width)
    val_blocks = vals_all.reshape(nblocks, blk, local_kv, width)
    sel_keys = key_blocks[idxc, :, kv_range]
    sel_vals = val_blocks[idxc, :, kv_range]
    valid = idx[0] >= 0
    keys = jnp.concatenate([sel_keys[0], kn[None, :, 0]], axis=0).reshape(-1, width)
    vals = jnp.concatenate([sel_vals[0], values[None, :, 0]], axis=0).reshape(-1, width)
    q_grp = jnp.transpose(qn, (1, 0, 2))
    do_grp = jnp.transpose(dout, (1, 0, 2))
    dq, dk, dv = block_grads(q_grp, do_grp, keys, vals, valid)
    dq_parts = jnp.transpose(dq, (1, 0, 2))
    tile = jnp.concatenate([dk, dv], axis=1).reshape(topk + 1, blk, 2 * width)
    tiles = [tile.astype(jnp.bfloat16)]
    tile_all = jnp.stack(tiles, axis=0)
    own = jnp.broadcast_to(position, (local_kv, 1))
    target = jnp.concatenate([idx, own], axis=1)
    count = lax.axis_size("ctx") * blk
    blocks = jnp.arange(count // blk, dtype=jnp.int32)
    onehot = (target[:, None, :] == blocks[None, :, None]).astype(jnp.bfloat16)
    term = jnp.einsum("gjs,gsbd->jbgd", onehot, tile_all, preferred_element_type=jnp.float32)
    dkv = lax.psum_scatter(
        term.reshape(count, local_kv, 2 * width).astype(jnp.bfloat16),
        "ctx",
        scatter_dimension=0,
        tiled=True,
    ).astype(jnp.float32)
    dkn = dkv[..., :width]
    dvalues = dkv[..., width:].astype(jnp.bfloat16)
    dq_raw, gq = norm_back(xq, rq, q_gain, dq_parts)
    dk_raw, gk = norm_back(xk, rk, k_gain, dkn)
    part_q = jnp.sum(gq.reshape(-1, width), axis=0)
    part_k = jnp.sum(gk.reshape(-1, width), axis=0)
    q_gain_grad, k_gain_grad = lax.psum((part_q, part_k), ("ctx", "head"))
    return (
        dq_raw.astype(jnp.bfloat16),
        dk_raw.astype(jnp.bfloat16),
        dvalues,
        q_gain_grad,
        k_gain_grad,
    )


def solution(mesh):
    return jax.shard_map(
        on_device,
        mesh=mesh,
        in_specs=(
            P("ctx", "head", None),
            P("ctx", "head", None),
            P("ctx", "head", None),
            P("ctx", "head", None),
            P(),
            P(),
            P("ctx", "head", None),
        ),
        out_specs=(
            P("ctx", "head", None),
            P("ctx", "head", None),
            P("ctx", "head", None),
            P(),
            P(),
        ),
        check_vma=False,
    )
```

profile of v0, /device:TPU:0, one launch (start us, length us, event | category | flops | bytes accessed | tf_op | source)
XLA Modules:
  0.0 631.9 jit_solution(6623182848136585088)
XLA Ops:
  20.2 39.6 %all-gather.3.cloned.1.call-done = bf16[16384,1,128]{2,0,1:T(8,128)(2,1)} async-done(((bf16[512,1,128]{2,0,1:T(8,128)(2,1)}), bf16[16384,1,128]{2,0,1:T(8,128)(2,1)}) %all-gather.3.cloned.1.call-update) | async-done | bytes 4194320 | tf_op jit(solution)/shard_map/all_gather | solution.py:64
  62.7 45.0 %all-gather.5.cloned.1.call-done = bf16[16384,1,128]{2,0,1:T(8,128)(2,1)} async-done(((bf16[512,1,128]{2,0,1:T(8,128)(2,1)}), bf16[16384,1,128]{2,0,1:T(8,128)(2,1)}) %all-gather.5.cloned.1.call-update) | async-done | bytes 4194320 | tf_op jit(solution)/shard_map/all_gather | solution.py:65
  114.2 330.0 %while.15 = (s32[]{:T(128)}, f32[4608,128]{1,0:T(8,128)}, f32[4608,128]{1,0:T(8,128)S(1)}, f32[8,512,128]{2,0,1:T(8,128)}, bf16[8,512,128]{2,1,0:T(8,128)(2,1)},...) while((s32[]{:T(128)}, f32[4608,128]{1,0:T(8,128)}, ...), condition=%wide.region_6.7_spmd.clone, body=%wide.region_2.6_spmd.clone.sunk | while | flops 3655399936 | bytes 235028752 | solution.py:49
  123.5 5.3 fusion.91
  137.9 8.0 %dynamic_update_slice.6 = f32[8,512,128]{2,0,1:T(8,128)} dynamic-update-slice(f32[8,512,128]{2,0,1:T(8,128)} %get-tuple-element.204, f32[1,512,128]{2,0,1:T(1,128)} %bitcast.91, s32[]{:T(128)} %get-tuple-element.201, s32[]{:T(128)} %constant.16.clone.1..sunk, s32[]{:T(128)} %constant.16.clone.1..sunk) | dynamic-update-slice | bytes 524292 | tf_op jit(solution)/shard_map/while/body/jit(dynamic_update_index_in_dim)/dynamic_update_slice | solution.py:49
  145.9 5.3 fusion.93
  164.3 5.3 fusion.91
  178.7 8.0 %dynamic_update_slice.6 = f32[8,512,128]{2,0,1:T(8,128)} dynamic-update-slice(f32[8,512,128]{2,0,1:T(8,128)} %get-tuple-element.204, f32[1,512,128]{2,0,1:T(1,128)} %bitcast.91, s32[]{:T(128)} %get-tuple-element.201, s32[]{:T(128)} %constant.16.clone.1..sunk, s32[]{:T(128)} %constant.16.clone.1..sunk) | dynamic-update-slice | bytes 524292 | tf_op jit(solution)/shard_map/while/body/jit(dynamic_update_index_in_dim)/dynamic_update_slice | solution.py:49
  186.7 6.1 fusion.93
  219.9 8.0 %dynamic_update_slice.6 = f32[8,512,128]{2,0,1:T(8,128)} dynamic-update-slice(f32[8,512,128]{2,0,1:T(8,128)} %get-tuple-element.204, f32[1,512,128]{2,0,1:T(1,128)} %bitcast.91, s32[]{:T(128)} %get-tuple-element.201, s32[]{:T(128)} %constant.16.clone.1..sunk, s32[]{:T(128)} %constant.16.clone.1..sunk) | dynamic-update-slice | bytes 524292 | tf_op jit(solution)/shard_map/while/body/jit(dynamic_update_index_in_dim)/dynamic_update_slice | solution.py:49
  228.0 6.1 fusion.93
  261.2 8.0 %dynamic_update_slice.6 = f32[8,512,128]{2,0,1:T(8,128)} dynamic-update-slice(f32[8,512,128]{2,0,1:T(8,128)} %get-tuple-element.204, f32[1,512,128]{2,0,1:T(1,128)} %bitcast.91, s32[]{:T(128)} %get-tuple-element.201, s32[]{:T(128)} %constant.16.clone.1..sunk, s32[]{:T(128)} %constant.16.clone.1..sunk) | dynamic-update-slice | bytes 524292 | tf_op jit(solution)/shard_map/while/body/jit(dynamic_update_index_in_dim)/dynamic_update_slice | solution.py:49
  269.2 6.1 fusion.93
  302.4 8.0 %dynamic_update_slice.6 = f32[8,512,128]{2,0,1:T(8,128)} dynamic-update-slice(f32[8,512,128]{2,0,1:T(8,128)} %get-tuple-element.204, f32[1,512,128]{2,0,1:T(1,128)} %bitcast.91, s32[]{:T(128)} %get-tuple-element.201, s32[]{:T(128)} %constant.16.clone.1..sunk, s32[]{:T(128)} %constant.16.clone.1..sunk) | dynamic-update-slice | bytes 524292 | tf_op jit(solution)/shard_map/while/body/jit(dynamic_update_index_in_dim)/dynamic_update_slice | solution.py:49
  310.5 6.1 fusion.93
  343.7 8.0 %dynamic_update_slice.6 = f32[8,512,128]{2,0,1:T(8,128)} dynamic-update-slice(f32[8,512,128]{2,0,1:T(8,128)} %get-tuple-element.204, f32[1,512,128]{2,0,1:T(1,128)} %bitcast.91, s32[]{:T(128)} %get-tuple-element.201, s32[]{:T(128)} %constant.16.clone.1..sunk, s32[]{:T(128)} %constant.16.clone.1..sunk) | dynamic-update-slice | bytes 524292 | tf_op jit(solution)/shard_map/while/body/jit(dynamic_update_index_in_dim)/dynamic_update_slice | solution.py:49
  351.7 6.1 fusion.93
  384.9 8.0 %dynamic_update_slice.6 = f32[8,512,128]{2,0,1:T(8,128)} dynamic-update-slice(f32[8,512,128]{2,0,1:T(8,128)} %get-tuple-element.204, f32[1,512,128]{2,0,1:T(1,128)} %bitcast.91, s32[]{:T(128)} %get-tuple-element.201, s32[]{:T(128)} %constant.16.clone.1..sunk, s32[]{:T(128)} %constant.16.clone.1..sunk) | dynamic-update-slice | bytes 524292 | tf_op jit(solution)/shard_map/while/body/jit(dynamic_update_index_in_dim)/dynamic_update_slice | solution.py:49
  393.0 6.1 fusion.93
  426.2 8.0 %dynamic_update_slice.6 = f32[8,512,128]{2,0,1:T(8,128)} dynamic-update-slice(f32[8,512,128]{2,0,1:T(8,128)} %get-tuple-element.204, f32[1,512,128]{2,0,1:T(1,128)} %bitcast.91, s32[]{:T(128)} %get-tuple-element.201, s32[]{:T(128)} %constant.16.clone.1..sunk, s32[]{:T(128)} %constant.16.clone.1..sunk) | dynamic-update-slice | bytes 524292 | tf_op jit(solution)/shard_map/while/body/jit(dynamic_update_index_in_dim)/dynamic_update_slice | solution.py:49
  434.2 6.1 fusion.93
  452.6 11.4 %copy.20 = bf16[32,512,1,256]{3,1,0,2:T(8,128)(2,1)} copy(bf16[32,512,1,256]{3,0,1,2:T(8,128)(2,1)} %convert_bitcast_fusion) | data formatting | bytes 16777216 | tf_op jit(solution)/shard_map/convert_element_type | solution.py:89
  470.1 86.1 %reduce-scatter.2.cloned.1.call-done = bf16[512,1,256]{2,0,1:T(8,128)(2,1)} async-done(((bf16[16384,1,256]{2,0,1:T(8,128)(2,1)}), bf16[512,1,256]{2,0,1:T(8,128)(2,1)}) %reduce-scatter.2.cloned.1.call-update) | async-done | bytes 262160 | tf_op jit(solution)/shard_map/reduce_scatter | solution.py:88
  557.4 64.7 %all-reduce.1 = (f32[128]{0:T(128)}, f32[128]{0:T(128)}) all-reduce(f32[128]{0:T(128)S(1)} %get-tuple-element.105, f32[128]{0:T(128)S(1)} %get-tuple-element.107), channel_id=1, replica_groups=mesh['ctx'=32,'head'=4] {'ctx','head'}, use_global_device_ids=true, to_apply=%region_11.12 | all-reduce | flops 256 | bytes 2048 | tf_op jit(solution)/shard_map/psum | solution.py:100
  (212 shorter events, 247.2 us)
Async XLA Ops:
  7.2 6.4 %copy-start.5 = (bf16[512,8,128]{2,1,0:T(8,128)(2,1)S(1)}, bf16[512,8,128]{2,1,0:T(8,128)(2,1)}, u32[]{:S(2)}) copy-start(bf16[512,8,128]{2,1,0:T(8,128)(2,1)} %param.9) | copy-start | bytes 3145732
  7.2 6.4 %copy-start.18 = (f32[128]{0:T(128)S(1)}, f32[128]{0:T(128)}, u32[]{:S(2)}) copy-start(f32[128]{0:T(128)} %param.13) | copy-start | bytes 1540
  7.2 52.6 %all-gather.3.cloned.1.call-start = ((), (), s32[]{:S(2)}) async-start(), calls=%async_computation.1 | async-start | bytes 4325376 | tf_op jit(solution)/shard_map/all_gather | solution.py:64
  8.4 9.6 %copy-start.14 = (f32[512]{0:T(512)}, f32[512]{0:T(512)S(1)}, u32[]{:S(2)}) copy-start(f32[512]{0:T(512)S(1)} %add_rsqrt_fusion.1) | copy-start | bytes 6148
  10.1 97.6 %all-gather.5.cloned.1.call-start = ((), (), s32[]{:S(2)}) async-start(), calls=%async_computation.2 | async-start | bytes 4325376 | tf_op jit(solution)/shard_map/all_gather | solution.py:65
  10.9 545.3 %reduce-scatter.2.cloned.1.call-start = ((), (), s32[]{:S(2)}) async-start(), calls=%async_computation.3 | async-start | bytes 8650752 | tf_op jit(solution)/shard_map/reduce_scatter | solution.py:88
  14.3 3.7 copy-start.11
  14.3 3.7 copy-start.16
  118.5 3.6 copy-start.2
  145.9 5.7 copy-start.1
  159.3 3.6 copy-start.2
  186.7 6.1 copy-start.1
  200.5 3.6 copy-start.2
  227.9 6.1 copy-start.1
  241.8 3.6 copy-start.2
  269.2 6.1 copy-start.1
  283.1 3.6 copy-start.2
  310.5 6.1 copy-start.1
  351.7 6.1 copy-start.1
  393.0 6.1 copy-start.1
  434.2 6.1 copy-start.1
  467.5 88.7 %copy-start.12 = (bf16[512,1,128]{2,0,1:T(8,128)(2,1)S(1)}, bf16[512,1,128]{2,0,1:T(8,128)(2,1)}, u32[]{:S(2)}) copy-start(bf16[512,1,128]{2,0,1:T(8,128)(2,1)} %param.10) | copy-start | bytes 393220
  467.5 88.7 %copy-start.15 = (f32[512]{0:T(512)S(1)}, f32[512]{0:T(512)}, u32[]{:S(2)}) copy-start(f32[512]{0:T(512)} %copy-done.14) | copy-start | bytes 6148
  467.5 88.7 %copy-start.17 = (f32[128]{0:T(128)S(1)}, f32[128]{0:T(128)}, u32[]{:S(2)}) copy-start(f32[128]{0:T(128)} %param.14) | copy-start | bytes 1540
  (36 other events, 96.5 us)
Sparse Core Ops, SparseCore 0:
  10.9 48.8 all-gather.2
  62.0 45.6 all-gather.4
  464.1 92.0 reduce-scatter.1
where the time goes:
time: 635 us; the launch traced here: 632 us
  matrix products  180 us (28%)
  waiting for transfers between devices  171 us (27%)
  local copies, waits for them, and re-layouts  128 us (20%)
  other arithmetic  73.3 us (12%)
  blocking collectives  64.7 us (10%)
  between operations  14 us (2%)
    reduce_scatter x1, waiting for transfers between devices, on_device(): lax.psum_scatter(term.reshape(count, local_kv, 2 * width).astype(jnp.bflo...  86.1 us
    psum x1, blocking collectives, on_device(): q_gain_grad, k_gain_grad = lax.psum((part_q, part_k), ('ctx', 'head'))  64.7 us
    dynamic_update_slice x8, local copies, waits for them, and re-layouts, block_grads(): (dk, dv), dq = lax.scan(one_head, (zeros, zeros), (q_grp, do_grp))  64.2 us
    dot_general x8, matrix products, one_head(): jnp.dot(dscores.T, qh, preferred_element_type=jnp.float32) * scale  48.1 us
    all_gather x1, waiting for transfers between devices, on_device(): lax.all_gather(values, 'ctx', axis=0, tiled=True)  45 us
    div x8, other arithmetic, one_head(): probs = expo / jnp.sum(expo, axis=1, keepdims=True)  42.6 us
    all_gather x1, waiting for transfers between devices, on_device(): lax.all_gather(kn, 'ctx', axis=0, tiled=True)  39.6 us
    while x80, local copies, waits for them, and re-layouts  36 us
  transfers between devices with their start and end apart: 3, of which 3 were waited for; matrix products, arithmetic and copies ran while one was open for 2% of the time, Pallas kernels for 0%

commit v1 on v0

v1 whole, which is shorter than its diff:
```python
import functools

import jax, jax.numpy as jnp
from jax import lax
from jax.experimental import pallas as pl
from jax.experimental.pallas import tpu as pltpu
from jax.sharding import PartitionSpec as P

SC = 128 ** -0.5
C2 = SC * 1.4426950408889634
NEG = -1e30
F32 = jnp.float32
BF = jnp.bfloat16

EPS = 1e-06


def norm_fwd(raw, gain):
    x = raw.astype(jnp.float32)
    scale_r = lax.rsqrt(jnp.mean(x * x, axis=-1, keepdims=True) + EPS)
    return (x, scale_r, (x * scale_r * gain).astype(jnp.bfloat16))


def norm_back(x, scale_r, gain, grad_y):
    along = gain * grad_y
    inner = jnp.mean(along * x, axis=-1, keepdims=True)
    grad_x = scale_r * (along - x * scale_r * scale_r * inner)
    return (grad_x, grad_y * x * scale_r)


def dot(a, b):
    return lax.dot_general(a, b, (((1,), (0,)), ((), ())), preferred_element_type=F32)

def fold(x, op):
    return op(x.reshape(x.shape[0] // 8, 8, x.shape[1]), axis=0)

def attn_kernel(idx_ref, kv_hbm, q_ref, qT_ref, do_ref, doT_ref,
                dq_ref, tile_ref, kg_ref,
                kb, vb, kT, vT, S, E, dk, dv, oT, dqT, mrow, drow, qs, dos, sem):
    H = q_ref.shape[0]
    J = 9
    me = lax.axis_index("ctx")
    cps = []
    for j in range(J):
        blk = jnp.maximum(idx_ref[j], 0) if j < 8 else me
        cps.append((pltpu.make_async_copy(kv_hbm.at[blk, :, 0:128], kb.at[j], sem.at[0, j]),
                    pltpu.make_async_copy(kv_hbm.at[blk, :, 128:256], vb.at[j], sem.at[1, j])))
    for a, b in cps:
        a.start(); b.start()
    for a, b in cps:
        a.wait(); b.wait()

    @pl.loop(0, J)
    def _(j):
        kT[j] = kb[j].T
        vT[j] = vb[j].T
        dk[j] = jnp.zeros(dk.shape[1:], F32)
        dv[j] = jnp.zeros(dv.shape[1:], F32)

    rows = lax.broadcasted_iota(jnp.int32, (512, 512), 0)
    cols = lax.broadcasted_iota(jnp.int32, (512, 512), 1)

    def A1(h, j, own):
        s = dot(kb[j], qT_ref[h])
        if own:
            s = jnp.where(rows <= cols, s, NEG)
        S[h % 2, j] = s
        cm = fold(s, jnp.max)
        if not own:
            cm = jnp.where(idx_ref[j] >= 0, cm, NEG)
        return cm

    def A2(h, j, own):
        m = mrow[h % 2]
        if not own:
            m = jnp.where(idx_ref[j] >= 0, m, 1e30)
        s = S[h % 2, j]
        e = jnp.exp2((s.reshape(64, 8, 512) - m[None]) * C2)
        l = jnp.sum(e, axis=0)
        eb = e.reshape(512, 512).astype(BF)
        E[h % 2, j] = eb
        oT[...] += dot(vT[j], eb)
        return l

    def C(h, j):
        dp = dot(vb[j], doT_ref[h])
        dl = drow[h % 2]
        dpb = (dp.reshape(64, 8, 512) - dl[None]).reshape(512, 512).astype(BF)
        eb = E[h % 2, j]
        ds = eb * dpb
        dv[j] += dot(eb, dos[h % 2])
        dk[j] += dot(ds, qs[h % 2])
        dqT[...] += dot(kT[j], ds)

    def step(t, a1, a2, c):
        if a2:
            oT[...] = jnp.zeros(oT.shape, F32)
        if c:
            dqT[...] = jnp.zeros(dqT.shape, F32)

        def body(j, carry, own=False):
            mx, l = carry
            if a1:
                mx = jnp.maximum(mx, A1(t, j, own))
            if a2:
                l = l + A2(t - 1, j, own)
            if c:
                C(t - 2, j)
            return mx, l
        carry = (jnp.full((8, 512), NEG, F32), jnp.zeros((8, 512), F32))
        carry = lax.fori_loop(0, J - 1, body, carry)
        mx, l = body(J - 1, carry, True)
        if c:
            h = t - 2
            rl = drow[h % 2 + 2]
            dq_ref[h] = (dqT[...] * (rl[:1] * SC)).T
        if a2:
            h = t - 1
            l1 = jnp.sum(l, axis=0, keepdims=True)
            rl = jnp.broadcast_to(1.0 / l1, (8, 512))
            o = oT[...]
            dl = jnp.sum(o * doT_ref[h].astype(F32), axis=0, keepdims=True) * rl[:1]
            drow[h % 2] = jnp.broadcast_to(dl, (8, 512))
            drow[h % 2 + 2] = rl
            rc = rl.T[:, :1]
            dos[h % 2] = (do_ref[h].astype(F32) * rc).astype(BF)
            qs[h % 2] = (q_ref[h].astype(F32) * (rc * SC)).astype(BF)
        if a1:
            m = jnp.max(mx, axis=0, keepdims=True)
            mrow[t % 2] = jnp.broadcast_to(m, (8, 512))

    step(0, True, False, False)
    step(1, True, True, False)

    @pl.loop(2, H)
    def _(t):
        step(t, True, True, True)
    step(H, False, True, True)
    step(H + 1, False, False, True)

    kg_ref[...] = jnp.zeros(kg_ref.shape, F32)

    @pl.loop(0, J)
    def _(j):
        kg_ref[...] += fold(dk[j] * kb[j].astype(F32), jnp.sum)
        tile_ref[j, :, 0:128] = dk[j].astype(BF)
        tile_ref[j, :, 128:256] = dv[j].astype(BF)


def attn(idx, kv_all, q, qT, do, doT):
    H = q.shape[0]
    V = functools.partial(pl.BlockSpec, memory_space=pltpu.VMEM)
    return pl.pallas_call(
        attn_kernel,
        out_shape=(
            jax.ShapeDtypeStruct((H, 512, 128), F32),
            jax.ShapeDtypeStruct((9, 512, 256), BF),
            jax.ShapeDtypeStruct((8, 128), F32),
        ),
        in_specs=[pl.BlockSpec(memory_space=pltpu.SMEM), pl.BlockSpec(memory_space=pl.ANY), V(), V(), V(), V()],
        out_specs=(V(), V(), V()),
        scratch_shapes=[
            pltpu.VMEM((9, 512, 128), BF), pltpu.VMEM((9, 512, 128), BF),
            pltpu.VMEM((9, 128, 512), BF), pltpu.VMEM((9, 128, 512), BF),
            pltpu.VMEM((2, 9, 512, 512), F32), pltpu.VMEM((2, 9, 512, 512), BF),
            pltpu.VMEM((9, 512, 128), F32), pltpu.VMEM((9, 512, 128), F32),
            pltpu.VMEM((128, 512), F32), pltpu.VMEM((128, 512), F32),
            pltpu.VMEM((2, 8, 512), F32), pltpu.VMEM((4, 8, 512), F32),
            pltpu.VMEM((2, 512, 128), BF), pltpu.VMEM((2, 512, 128), BF),
            pltpu.SemaphoreType.DMA((2, 9)),
        ],
        compiler_params=pltpu.CompilerParams(vmem_limit_bytes=60 * 2 ** 20),
    )(idx, kv_all, q, qT, do, doT)


def on_device(q_raw, k_raw, values, dout, q_gain, k_gain, chosen):
    blk, heads, width = q_raw.shape
    position = lax.axis_index("ctx")
    k2, v2 = k_raw.reshape(blk, width), values.reshape(blk, width)
    xk, rk, kn = norm_fwd(k2, k_gain)
    kv_all = lax.all_gather(jnp.concatenate([kn, v2], axis=1), "ctx", axis=0)
    xq, rq, qn = norm_fwd(jnp.transpose(q_raw, (1, 0, 2)), q_gain)
    do = jnp.transpose(dout, (1, 0, 2))
    idx = chosen.reshape(-1)
    dq, tile, kg = attn(idx, kv_all, qn, jnp.swapaxes(qn, 1, 2), do, jnp.swapaxes(do, 1, 2))
    dq_raw, gq = norm_back(xq, rq, q_gain, dq)
    part_q = jnp.sum(gq.reshape(-1, width), axis=0)
    part_k = jnp.sum(kg, axis=0) / k_gain
    q_gain_grad, k_gain_grad = lax.psum((part_q, part_k), ("ctx", "head"))
    target = jnp.concatenate([idx, position[None]])
    onehot = target[None, :] == jnp.arange(32, dtype=jnp.int32)[:, None]
    slot = jnp.argmax(onehot, axis=1)
    hit = jnp.any(onehot, axis=1)
    term = jnp.where(hit[:, None, None], tile[slot], 0).reshape(32 * blk, 2 * width)
    dkv = lax.psum_scatter(term, "ctx", scatter_dimension=0, tiled=True).astype(F32)
    dk_raw, _ = norm_back(xk, rk, k_gain, dkv[:, :width])
    return (
        jnp.transpose(dq_raw.astype(BF), (1, 0, 2)),
        dk_raw.astype(BF).reshape(blk, 1, width),
        dkv[:, width:].astype(BF).reshape(blk, 1, width),
        q_gain_grad,
        k_gain_grad,
    )


def solution(mesh):
    tok = P("ctx", "head", None)
    return jax.shard_map(
        on_device,
        mesh=mesh,
        in_specs=(tok, tok, tok, tok, P(), P(), tok),
        out_specs=(tok, tok, tok, P(), P()),
        check_vma=False,
    )
```

time: 635 us -> 277 us (0.44)
  matrix products: 180 us -> 0 us
  local copies, waits for them, and re-layouts: 128 us -> 18.4 us
  waiting for transfers between devices: 171 us -> 66.9 us
  Pallas kernels: 0 us -> 91.1 us
  other arithmetic: 73.3 us -> 19.9 us
    dot_general x49 -> x0, matrix products: 180 us -> none  [the longest x8 48.1 us: one_head(): jnp.dot(dscores.T, qh, preferred_element_type=jnp.float32) * scale]
    pallas_call x0 -> x1, Pallas kernels: none -> 91.1 us  [attn(): pl.pallas_call(attn_kernel, out_shape=(jax.ShapeDtypeStruct((H, 512, 128)...]
    reduce_scatter x1, waiting for transfers between devices: 86.1 us -> 20.1 us  [on_device(): lax.psum_scatter(term, 'ctx', scatter_dimension=0, tiled=True).astype(F32)]
    dynamic_update_slice x8 -> x0, local copies, waits for them, and re-layouts: 64.2 us -> none  [block_grads(): (dk, dv), dq = lax.scan(one_head, (zeros, zeros), (q_grp, do_grp))]
    div x8 -> x1, other arithmetic: 42.6 us -> 0.01 us  [on_device(): part_k = jnp.sum(kg, axis=0) / k_gain]
    all_gather x2 -> x1, waiting for transfers between devices: 84.6 us -> 46.8 us  [on_device(): kv_all = lax.all_gather(jnp.concatenate([kn, v2], axis=1), 'ctx', axis=0)]
    while x80 -> x0, local copies, waits for them, and re-layouts: 36 us -> none
    reduce_sum x9 -> x2, other arithmetic: 12.4 us -> 1.07 us  [the longest x1 1.05 us: norm_back(): inner = jnp.mean(along * x, axis=-1, keepdims=True)]
  transfers between devices with their start and end apart: 3 -> 2, of which waited for: 3 -> 2; matrix products, arithmetic and copies ran while one was open for 2% -> 6% of each run, Pallas kernels for 0% -> 0%
where the time goes in v1:
time: 277 us; the launch traced here: 276 us
  Pallas kernels  91.1 us (33%)
  waiting for transfers between devices  66.9 us (24%)
  blocking collectives  65.5 us (24%)
  other arithmetic  19.9 us (7%)
  local copies, waits for them, and re-layouts  18.4 us (7%)
  between operations  14.2 us (5%)
    pallas_call x1, Pallas kernels, attn(): pl.pallas_call(attn_kernel, out_shape=(jax.ShapeDtypeStruct((H, 512, 128)...  91.1 us
    psum x1, blocking collectives, on_device(): q_gain_grad, k_gain_grad = lax.psum((part_q, part_k), ('ctx', 'head'))  65.5 us
    all_gather x1, waiting for transfers between devices, on_device(): kv_all = lax.all_gather(jnp.concatenate([kn, v2], axis=1), 'ctx', axis=0)  46.8 us
    reduce_scatter x1, waiting for transfers between devices, on_device(): lax.psum_scatter(term, 'ctx', scatter_dimension=0, tiled=True).astype(F32)  20.1 us
    select_n x1, other arithmetic, on_device(): jnp.where(hit[:, None, None], tile[slot], 0).reshape(32 * blk, 2 * width)  8.01 us
    unnamed x20, local copies, waits for them, and re-layouts  7.17 us
    gather x1, local copies, waits for them, and re-layouts, on_device(): tile[slot]  6.39 us
  transfers between devices with their start and end apart: 2, of which 2 were waited for; matrix products, arithmetic and copies ran while one was open for 6% of the time, Pallas kernels for 0%

profile of v1, /device:TPU:0, one launch (start us, length us, event | category | flops | bytes accessed | tf_op | source)
XLA Modules:
  0.0 276.0 jit_solution(5432011254771330520)
XLA Ops:
  7.2 1.1 fusion.26
  8.4 1.0 fusion.21
  9.4 1.6 pad_maximum_fusion
  11.1 2.4 copy.28
  13.6 1.5 copy.21
  15.0 0.7 copy.19
  15.7 0.2 fusion.11
  16.0 0.3 fusion.6
  16.3 1.3 copy.22.q_ref
  17.9 0.6 iota_reduce_fusion
  18.5 1.4 fusion.17.qT_ref
  20.0 46.8 %all-gather.3.cloned.1.call-done = bf16[16384,256]{1,0:T(8,128)(2,1)} async-done(((bf16[512,256]{1,0:T(8,128)(2,1)}), bf16[16384,256]{1,0:T(8,128)(2,1)}) %all-gather.3.cloned.1.call-update) | async-done | bytes 8388624 | tf_op jit(solution)/shard_map/all_gather | solution.py:181
  66.7 91.1 %shard_map.110 = (f32[8,512,128]{2,1,0:T(8,128)}, bf16[9,512,256]{2,1,0:T(8,128)(2,1)}, f32[8,128]{1,0:T(8,128)}) custom-call(s32[8]{0:T(128)} %bitcast.72, bf16[32,512,256]{2,1,0:T(8,128)(2,1)} %bitcast.67, bf16[8,512,128]{2,1,0:T(8,128)(2,1)} %copy.22.q_ref, bf16[8,128,512]{2,1,0:T(8,128)(2,1)} %fusion.17.qT_ref, bf16[8,512,128]{2,1,0:T(8,128)(2,1)} %bitcast.68, ...), custom_call_target="tpu_custom_call" | custom-call | tf_op jit(solution)/shard_map/pallas_call | solution.py:153
  157.9 6.4 %gather_fusion = bf16[32,512,256]{2,1,0:T(8,128)(2,1)} fusion(bf16[9,512,256]{2,1,0:T(8,128)(2,1)} %get-tuple-element.10, s32[1024]{0:T(1024)S(1)} %pad_clamp_fusion), kind=kCustom, calls=%fused_computation | custom fusion | bytes 16777344 | tf_op jit(solution)/shard_map/gather | solution.py:194
  164.2 8.0 %bitcast_select_fusion = bf16[16384,256]{1,0:T(8,128)(2,1)} fusion(bf16[32,512,256]{2,1,0:T(8,128)(2,1)} %gather_fusion, pred[16384]{0:T(1024)(128)(4,1)S(1)} %bitcast.71), kind=kLoop, calls=%fused_computation.1 | loop fusion | flops 4194304 | bytes 16793600 | tf_op jit(solution)/shard_map/jit(_where)/select_n | solution.py:194
  172.3 1.9 copy.23
  174.2 0.9 fusion.14
  175.1 1.6 fusion.18
  176.7 2.5 copy.25
  179.2 65.5 %all-reduce = (f32[128]{0:T(128)}, f32[128]{0:T(128)}) all-reduce(f32[128]{0:T(128)S(1)} %get-tuple-element.23, f32[128]{0:T(128)S(1)} %div.19), channel_id=1, replica_groups=mesh['ctx'=32,'head'=4] {'ctx','head'}, use_global_device_ids=true, to_apply=%region_8.9 | all-reduce | flops 256 | bytes 2048 | tf_op jit(solution)/shard_map/psum | solution.py:189
  244.7 20.1 %reduce-scatter.2.cloned.1.call-done = bf16[512,256]{1,0:T(8,128)(2,1)} async-done(((bf16[16384,256]{1,0:T(8,128)(2,1)}), bf16[512,256]{1,0:T(8,128)(2,1)}) %reduce-scatter.2.cloned.1.call-update) | async-done | bytes 262160 | tf_op jit(solution)/shard_map/reduce_scatter | solution.py:195
  264.8 1.1 fusion.27
  265.9 1.6 slice_bitcast_fusion
  267.4 1.8 fusion.28
  (30 shorter events, 0.5 us)
Async XLA Ops:
  7.2 6.4 %copy-start = (bf16[512,8,128]{2,1,0:T(8,128)(2,1)S(1)}, bf16[512,8,128]{2,1,0:T(8,128)(2,1)}, u32[]{:S(2)}) copy-start(bf16[512,8,128]{2,1,0:T(8,128)(2,1)} %param.10) | copy-start | bytes 3145732
  7.2 59.5 %all-gather.3.cloned.1.call-start = ((), (), s32[]{:S(2)}) async-start(), calls=%async_computation.2 | async-start | bytes 8650752 | tf_op jit(solution)/shard_map/all_gather | solution.py:181
  11.1 4.0 %copy-start.2 = (bf16[512,8,128]{2,1,0:T(8,128)(2,1)S(1)}, bf16[512,8,128]{2,1,0:T(8,128)(2,1)}, u32[]{:S(2)}) copy-start(bf16[512,8,128]{2,1,0:T(8,128)(2,1)} %param.7) | copy-start | bytes 3145732
  11.1 253.7 %reduce-scatter.2.cloned.1.call-start = ((), (), s32[]{:S(2)}) async-start(), calls=%async_computation.1 | async-start | bytes 8650752 | tf_op jit(solution)/shard_map/reduce_scatter | solution.py:195
  15.0 0.9 copy-start.3
  16.0 1.7 copy-start.6
  176.7 2.5 copy-start.5
  176.7 2.5 copy-start.4
  176.7 88.1 %copy-start.1 = (bf16[512,1,128]{2,0,1:T(8,128)(2,1)S(1)}, bf16[512,1,128]{2,0,1:T(8,128)(2,1)}, u32[]{:S(2)}) copy-start(bf16[512,1,128]{2,0,1:T(8,128)(2,1)} %param.8) | copy-start | bytes 393220
Sparse Core Ops, SparseCore 0:
  11.2 55.4 all-gather.2
  172.4 92.3 reduce-scatter.1

commit v2 on v1

--- a/solution.py
+++ b/solution.py
@@ -139,12 +139,190 @@
     step(H + 1, False, False, True)
 
     kg_ref[...] = jnp.zeros(kg_ref.shape, F32)
+    tile_ref[J] = jnp.zeros(tile_ref.shape[1:], BF)
 
     @pl.loop(0, J)
     def _(j):
         kg_ref[...] += fold(dk[j] * kb[j].astype(F32), jnp.sum)
         tile_ref[j, :, 0:128] = dk[j].astype(BF)
         tile_ref[j, :, 128:256] = dv[j].astype(BF)
+
+
+MESH = pl.DeviceIdType.MESH
+
+
+def place():
+    ctx, y = lax.axis_index("ctx"), lax.axis_index("head")
+    return ctx // 8, (ctx // 2) % 4, ctx % 2, y
+
+
+def peer(z, x, c, y):
+    return (z * 8 + x * 2 + c, y)
+
+
+def greet(devices):
+    barrier = pltpu.get_barrier_semaphore()
+    for d in devices:
+        pl.semaphore_signal(barrier, inc=1, device_id=d, device_id_type=MESH)
+    pl.semaphore_wait(barrier, len(devices))
+
+
+def scatter_kernel(slot_ref, tile_ref, g_ref, dk_ref, dv_ref, gout_ref,
+                   A, B, cur, R1, R2, T, Q1, Q2, GS, GZ, GX, GY,
+                   s0, r0, s1, r1, s2, r2, sg, rg):
+    z, x, c, y = place()
+
+    def along(axis, off):
+        if axis == "z":
+            return peer((z + off) % 4, x, c, y)
+        if axis == "x":
+            return peer(z, (x + off) % 4, c, y)
+        return peer(z, x, c, (y + off) % 4)
+
+    sib = peer(z, x, 1 - c, y)
+    greet([sib] + [along(a, o) for a in "zxy" for o in (1, 2, 3)])
+    pending = []
+
+    def send(src, dst, ss, rs, to):
+        cp = pltpu.make_async_remote_copy(src_ref=src, dst_ref=dst, send_sem=ss, recv_sem=rs,
+                                          device_id=to, device_id_type=MESH)
+        cp.start()
+        pending.append(cp)
+        return cp
+
+    gcp = send(g_ref, GS, sg.at[0], rg.at[0], sib)
+
+    axes = (("z", "x"), ("x", "z"))
+    coord = {"z": z, "x": x}
+
+    def block(half, u, w, cc):
+        return (u * 8 + w * 2 + cc) if half == 0 else (w * 8 + u * 2 + cc)
+
+    def cols(half):
+        return slice(half * 128, half * 128 + 128)
+
+    first = {}
+    for off in (2, 1, 3, 0):
+        for half in (0, 1):
+            u = (coord[axes[half][0]] + off) % 4
+
+            @pl.loop(0, 4)
+            def _(w):
+                A[half, off, w] = tile_ref[slot_ref[block(half, u, w, 1 - c)], :, cols(half)]
+            first[half, off] = send(A.at[half, off], B.at[half, off], s0.at[half * 4 + off], r0.at[half * 4 + off], sib)
+
+    def group(G, base, kind):
+        me = {"z": z, "x": x, "y": y}[kind]
+        cps = [send(G.at[me], G.at[me], sg.at[base + o], rg.at[base + o], along(kind, o)) for o in (1, 2, 3)]
+        return cps
+
+    def gsum(G, cps):
+        for cp in cps:
+            cp.wait_recv()
+        return (G[0] + G[1]) + (G[2] + G[3])
+
+    def own_sum(half, off):
+        first[half, off].wait_recv()
+        u = (coord[axes[half][0]] + off) % 4
+
+        @pl.loop(0, 4)
+        def _(w):
+            mine = tile_ref[slot_ref[block(half, u, w, c)], :, cols(half)]
+            cur[half, off, w] = (mine.astype(F32) + B[half, off, w].astype(F32)).astype(BF)
+
+    def s1send(k, half, src, dst, off):
+        return send(src, dst, s1.at[half, k], r1.at[half, k], along(axes[half][0], off))
+
+    c1 = {}
+    for half in (0, 1):
+        own_sum(half, 2)
+        c1[half, 0] = s1send(0, half, cur.at[half, 2, 0:2], R1.at[half, 0], 1)
+        c1[half, 1] = s1send(1, half, cur.at[half, 2, 2:4], R1.at[half, 1], 3)
+    for half in (0, 1):
+        own_sum(half, 1)
+        c1[half, 2] = s1send(2, half, cur.at[half, 1, 2:4], R2.at[half, 0, 2:4], 1)
+        own_sum(half, 3)
+        c1[half, 3] = s1send(3, half, cur.at[half, 3, 0:2], R2.at[half, 1, 0:2], 3)
+    gcp.wait_recv()
+    GZ[z] = g_ref[...] + GS[...]
+    gz = group(GZ, 0, "z")
+    for half in (0, 1):
+        own_sum(half, 0)
+    for half in (0, 1):
+        c1[half, 0].wait_recv()
+
+        @pl.loop(0, 2)
+        def _(w):
+            cur[half, 1, w] = (cur[half, 1, w].astype(F32) + R1[half, 0, w].astype(F32)).astype(BF)
+        c1[half, 4] = s1send(4, half, cur.at[half, 1, 0:2], R2.at[half, 0, 0:2], 1)
+        c1[half, 1].wait_recv()
+
+        @pl.loop(0, 2)
+        def _(w):
+            cur[half, 3, w + 2] = (cur[half, 3, w + 2].astype(F32) + R1[half, 1, w].astype(F32)).astype(BF)
+        c1[half, 5] = s1send(5, half, cur.at[half, 3, 2:4], R2.at[half, 1, 2:4], 3)
+    GX[x] = gsum(GZ, gz)
+    gx = group(GX, 3, "x")
+
+    def s2send(k, half, src, dst, off):
+        return send(src, dst, s2.at[half, k], r2.at[half, k], along(axes[half][1], off))
+
+    lo, hi = slice(0, 256), slice(256, 512)
+    c2 = {}
+    for half in (0, 1):
+        for k in (2, 3, 4, 5):
+            c1[half, k].wait_recv()
+        cw = coord[axes[half][1]]
+
+        @pl.loop(0, 4)
+        def _(o):
+            w = (cw + o) % 4
+            T[half, o] = (cur[half, 0, w].astype(F32) + R2[half, 0, w].astype(F32)
+                          + R2[half, 1, w].astype(F32)).astype(BF)
+        c2[half, 0] = s2send(0, half, T.at[half, 2, lo], Q1.at[half, 0], 1)
+        c2[half, 1] = s2send(1, half, T.at[half, 2, hi], Q1.at[half, 1], 3)
+        c2[half, 2] = s2send(2, half, T.at[half, 1, hi], Q2.at[half, 0, hi], 1)
+        c2[half, 3] = s2send(3, half, T.at[half, 3, lo], Q2.at[half, 1, lo], 3)
+    GY[y] = gsum(GX, gx)
+    gy = group(GY, 6, "y")
+    for half in (0, 1):
+        c2[half, 0].wait_recv()
+        T[half, 1, lo] = (T[half, 1, lo].astype(F32) + Q1[half, 0].astype(F32)).astype(BF)
+        c2[half, 4] = s2send(4, half, T.at[half, 1, lo], Q2.at[half, 0, lo], 1)
+        c2[half, 1].wait_recv()
+        T[half, 3, hi] = (T[half, 3, hi].astype(F32) + Q1[half, 1].astype(F32)).astype(BF)
+        c2[half, 5] = s2send(5, half, T.at[half, 3, hi], Q2.at[half, 1, hi], 3)
+    gout_ref[...] = gsum(GY, gy)
+    for half in (0, 1):
+        for k in (2, 3, 4, 5):
+            c2[half, k].wait_recv()
+        out = T[half, 0].astype(F32) + Q2[half, 0].astype(F32) + Q2[half, 1].astype(F32)
+        if half == 0:
+            dk_ref[...] = out
+        else:
+            dv_ref[...] = out.astype(BF)
+    for cp in pending:
+        cp.wait_send()
+
+
+def scatter(slot, tile, g):
+    V = functools.partial(pl.BlockSpec, memory_space=pltpu.VMEM)
+    D = pltpu.SemaphoreType.DMA
+    return pl.pallas_call(
+        scatter_kernel,
+        out_shape=(jax.ShapeDtypeStruct((512, 128), F32), jax.ShapeDtypeStruct((512, 128), BF),
+                   jax.ShapeDtypeStruct((8, 128), F32)),
+        in_specs=[pl.BlockSpec(memory_space=pltpu.SMEM), V(), V()],
+        out_specs=(V(), V(), V()),
+        scratch_shapes=[
+            pltpu.VMEM((2, 4, 4, 512, 128), BF), pltpu.VMEM((2, 4, 4, 512, 128), BF), pltpu.VMEM((2, 4, 4, 512, 128), BF),
+            pltpu.VMEM((2, 2, 2, 512, 128), BF), pltpu.VMEM((2, 2, 4, 512, 128), BF),
+            pltpu.VMEM((2, 4, 512, 128), BF), pltpu.VMEM((2, 2, 256, 128), BF), pltpu.VMEM((2, 2, 512, 128), BF),
+            pltpu.VMEM((8, 128), F32), pltpu.VMEM((4, 8, 128), F32), pltpu.VMEM((4, 8, 128), F32), pltpu.VMEM((4, 8, 128), F32),
+            D((8,)), D((8,)), D((2, 6)), D((2, 6)), D((2, 6)), D((2, 6)), D((10,)), D((10,)),
+        ],
+        compiler_params=pltpu.CompilerParams(collective_id=1, has_side_effects=True, vmem_limit_bytes=48 * 2 ** 20),
+    )(slot, tile, g)
 
 
 def attn(idx, kv_all, q, qT, do, doT):
@@ -154,7 +332,7 @@
         attn_kernel,
         out_shape=(
             jax.ShapeDtypeStruct((H, 512, 128), F32),
-            jax.ShapeDtypeStruct((9, 512, 256), BF),
+            jax.ShapeDtypeStruct((10, 512, 256), BF),
             jax.ShapeDtypeStruct((8, 128), F32),
         ),
         in_specs=[pl.BlockSpec(memory_space=pltpu.SMEM), pl.BlockSpec(memory_space=pl.ANY), V(), V(), V(), V()],
@@ -186,20 +364,18 @@
     dq_raw, gq = norm_back(xq, rq, q_gain, dq)
     part_q = jnp.sum(gq.reshape(-1, width), axis=0)
     part_k = jnp.sum(kg, axis=0) / k_gain
-    q_gain_grad, k_gain_grad = lax.psum((part_q, part_k), ("ctx", "head"))
     target = jnp.concatenate([idx, position[None]])
-    onehot = target[None, :] == jnp.arange(32, dtype=jnp.int32)[:, None]
-    slot = jnp.argmax(onehot, axis=1)
-    hit = jnp.any(onehot, axis=1)
-    term = jnp.where(hit[:, None, None], tile[slot], 0).reshape(32 * blk, 2 * width)
-    dkv = lax.psum_scatter(term, "ctx", scatter_dimension=0, tiled=True).astype(F32)
-    dk_raw, _ = norm_back(xk, rk, k_gain, dkv[:, :width])
+    match = target[None, :] == jnp.arange(32, dtype=jnp.int32)[:, None]
+    slot = jnp.min(jnp.where(match, jnp.arange(9, dtype=jnp.int32)[None, :], 9), axis=1)
+    parts = jnp.concatenate([part_q[None], part_k[None], jnp.zeros((6, width), F32)], axis=0)
+    dkn, dvalues, gains = scatter(slot, tile, parts)
+    dk_raw, _ = norm_back(xk, rk, k_gain, dkn)
     return (
         jnp.transpose(dq_raw.astype(BF), (1, 0, 2)),
         dk_raw.astype(BF).reshape(blk, 1, width),
-        dkv[:, width:].astype(BF).reshape(blk, 1, width),
-        q_gain_grad,
-        k_gain_grad,
+        dvalues.reshape(blk, 1, width),
+        gains[0],
+        gains[1],
     )
 
 

time: 277 us -> 211 us (0.76)
  blocking collectives: 65.5 us -> 0 us
  Pallas kernels: 91.1 us -> 127 us
  waiting for transfers between devices: 66.9 us -> 47.5 us
  other arithmetic: 19.9 us -> 10.5 us
  local copies, waits for them, and re-layouts: 18.4 us -> 11.6 us
    psum x1 -> x0, blocking collectives: 65.5 us -> none  [on_device(): q_gain_grad, k_gain_grad = lax.psum((part_q, part_k), ('ctx', 'head'))]
    pallas_call x0 -> x1, Pallas kernels: none -> 35.3 us  [scatter(): pl.pallas_call(scatter_kernel, out_shape=(jax.ShapeDtypeStruct((512, 128)...]
    reduce_scatter x1 -> x0, waiting for transfers between devices: 20.1 us -> none  [on_device(): lax.psum_scatter(term, 'ctx', scatter_dimension=0, tiled=True).astype(F32)]
    select_n x2 -> x0, other arithmetic: 8.01 us -> none  [the longest x1 8.01 us: on_device(): jnp.where(hit[:, None, None], tile[slot], 0).reshape(32 * blk, 2 * width)]
    gather x1 -> x0, local copies, waits for them, and re-layouts: 6.39 us -> none  [on_device(): tile[slot]]
    unnamed x20 -> x27, local copies, waits for them, and re-layouts: 7.17 us -> 6.78 us
  transfers between devices with their start and end apart: 2 -> 1, of which waited for: 2 -> 1; matrix products, arithmetic and copies ran while one was open for 6% -> 4% of each run, Pallas kernels for 0% -> 0%
where the time goes in v2:
time: 211 us
  Pallas kernels  127 us (60%)
  waiting for transfers between devices  47.5 us (23%)
  between operations  14.2 us (7%)
  local copies, waits for them, and re-layouts  11.6 us (5%)
  other arithmetic  10.5 us (5%)
    pallas_call x1, Pallas kernels, attn(): pl.pallas_call(attn_kernel, out_shape=(jax.ShapeDtypeStruct((H, 512, 128)...  91.3 us
    all_gather x1, waiting for transfers between devices, on_device(): kv_all = lax.all_gather(jnp.concatenate([kn, v2], axis=1), 'ctx', axis=0)  47.5 us
    pallas_call x1, Pallas kernels, scatter(): pl.pallas_call(scatter_kernel, out_shape=(jax.ShapeDtypeStruct((512, 128)...  35.3 us
    unnamed x27, local copies, waits for them, and re-layouts  6.78 us
  transfers between devices with their start and end apart: 1, of which 1 were waited for; matrix products, arithmetic and copies ran while one was open for 4% of the time, Pallas kernels for 0%

profile of v2, /device:TPU:0, one launch (start us, length us, event | category | flops | bytes accessed | tf_op | source)
XLA Modules:
  0.0 210.6 jit_solution(17218259171590231533)
XLA Ops:
  7.2 1.1 fusion.26
  8.4 1.0 fusion.21
  9.4 1.6 pad_maximum_fusion
  11.1 2.5 %copy.27 = bf16[512,8,128]{2,0,1:T(8,128)(2,1)} copy(bf16[512,8,128]{2,1,0:T(8,128)(2,1)} %param.10) | data formatting | bytes 2097152 | tf_op args[3]
  13.6 1.5 copy.21
  15.0 0.7 copy.19
  15.7 0.2 fusion.11
  16.0 0.3 fusion.6
  16.4 1.3 copy.22.q_ref
  17.7 0.1 pad.2.clone
  17.7 0.1 pad_add_fusion
  17.8 0.1 select_reduce_fusion.slot_ref
  17.9 1.3 fusion.17.qT_ref
  19.2 47.5 %all-gather.3.cloned.1.call-done = bf16[16384,256]{1,0:T(8,128)(2,1)} async-done(((bf16[512,256]{1,0:T(8,128)(2,1)}), bf16[16384,256]{1,0:T(8,128)(2,1)}) %all-gather.3.cloned.1.call-update) | async-done | bytes 8388624 | tf_op jit(solution)/shard_map/all_gather | solution.py:359
  66.7 91.3 %shard_map.110 = (f32[8,512,128]{2,1,0:T(8,128)}, bf16[10,512,256]{2,1,0:T(8,128)(2,1)}, f32[8,128]{1,0:T(8,128)}) custom-call(s32[8]{0:T(128)} %bitcast.74, bf16[32,512,256]{2,1,0:T(8,128)(2,1)} %bitcast.69, bf16[8,512,128]{2,1,0:T(8,128)(2,1)} %copy.22.q_ref, bf16[8,128,512]{2,1,0:T(8,128)(2,1)} %fusion.17.qT_ref, bf16[8,512,128]{2,1,0:T(8,128)(2,1)} %bitcast.70, ...), custom_call_target="tpu_custom_call" | custom-call | tf_op jit(solution)/shard_map/pallas_call | solution.py:331
  158.0 2.9 %copy.23 = f32[8,512,128]{1,2,0:T(8,128)} copy(f32[8,512,128]{2,1,0:T(8,128)} %get-tuple-element.11) | data formatting | bytes 4194304 | tf_op jit(solution)/shard_map/pallas_call | solution.py:331
  161.0 2.9 %fusion.14 = (f32[128]{0:T(128)S(1)}, f32[8,512]{1,0:T(8,128)S(1)}) fusion(f32[8,512,128]{1,2,0:T(8,128)} %copy.23, bf16[512,8,128]{0,2,1:T(8,128)(2,1)} %copy-done.1, f32[8,512]{1,0:T(8,128)S(1)} %add_rsqrt_fusion, f32[128]{0:T(128)S(1)} %copy-done.7), kind=kLoop, calls=%fused_computation.16 | loop fusion | flops 3665792 | bytes 3179520 | tf_op jit(solution)/shard_map/reduce_sum | solution.py:365
  164.1 35.3 %shard_map.111 = (f32[512,128]{1,0:T(8,128)S(1)}, bf16[512,128]{1,0:T(8,128)(2,1)S(1)}, f32[8,128]{1,0:T(8,128)S(1)}) custom-call(s32[32]{0:T(128)S(1)} %select_reduce_fusion.slot_ref, bf16[10,512,256]{2,1,0:T(8,128)(2,1)S(1)} %copy-done, f32[8,128]{1,0:T(8,128)S(1)} %maximum_maximum_fusion.g_ref), custom_call_target="tpu_custom_call" | custom-call | tf_op jit(solution)/shard_map/pallas_call | solution.py:311
  199.4 0.1 fusion.27
  199.6 0.9 fusion.28
  200.5 0.5 slice_bitcast_fusion
  201.0 0.6 fusion.18
  201.6 1.5 copy.25
  203.1 0.7 copy.29
  (32 shorter events, 0.2 us)
Async XLA Ops:
  7.2 6.4 %copy-start.4 = (bf16[512,8,128]{2,1,0:T(8,128)(2,1)S(1)}, bf16[512,8,128]{2,1,0:T(8,128)(2,1)}, u32[]{:S(2)}) copy-start(bf16[512,8,128]{2,1,0:T(8,128)(2,1)} %param.10) | copy-start | bytes 3145732
  7.2 59.5 %all-gather.3.cloned.1.call-start = ((), (), s32[]{:S(2)}) async-start(), calls=%async_computation | async-start | bytes 8650752 | tf_op jit(solution)/shard_map/all_gather | solution.py:359
  11.1 4.0 %copy-start.6 = (bf16[512,8,128]{2,1,0:T(8,128)(2,1)S(1)}, bf16[512,8,128]{2,1,0:T(8,128)(2,1)}, u32[]{:S(2)}) copy-start(bf16[512,8,128]{2,1,0:T(8,128)(2,1)} %param.7) | copy-start | bytes 3145732
  15.0 1.0 copy-start.7
  15.7 2.2 %copy-start.1 = (bf16[512,8,128]{0,2,1:T(8,128)(2,1)}, bf16[512,8,128]{0,2,1:T(8,128)(2,1)S(1)}, u32[]{:S(2)}) copy-start(bf16[512,8,128]{0,2,1:T(8,128)(2,1)S(1)} %copy.19) | copy-start | bytes 3145732
  16.0 1.7 copy-start.10
  161.0 3.0 %copy-start.9 = (f32[8,128]{1,0:T(8,128)S(1)}, f32[8,128]{1,0:T(8,128)}, u32[]{:S(2)}) copy-start(f32[8,128]{1,0:T(8,128)} %get-tuple-element.13) | copy-start | bytes 12292
  161.0 3.0 %copy-start.8 = (f32[128]{0:T(128)S(1)}, f32[128]{0:T(128)}, u32[]{:S(2)}) copy-start(f32[128]{0:T(128)} %param.12) | copy-start | bytes 1540
  161.0 3.1 %copy-start = (bf16[10,512,256]{2,1,0:T(8,128)(2,1)S(1)}, bf16[10,512,256]{2,1,0:T(8,128)(2,1)}, u32[]{:S(2)}) copy-start(bf16[10,512,256]{2,1,0:T(8,128)(2,1)} %get-tuple-element.12.tile_ref) | copy-start | bytes 7864324
  163.9 35.5 %copy-start.5 = (bf16[512,1,128]{2,0,1:T(8,128)(2,1)S(1)}, bf16[512,1,128]{2,0,1:T(8,128)(2,1)}, u32[]{:S(2)}) copy-start(bf16[512,1,128]{2,0,1:T(8,128)(2,1)} %param.8) | copy-start | bytes 393220
  164.0 37.0 %copy-start.2 = (bf16[512,8,128]{0,2,1:T(8,128)(2,1)S(1)}, bf16[512,8,128]{0,2,1:T(8,128)(2,1)}, u32[]{:S(2)}) copy-start(bf16[512,8,128]{0,2,1:T(8,128)(2,1)} %copy-done.1) | copy-start | bytes 3145732
  164.0 37.0 %copy-start.3 = (f32[8,512,128]{1,2,0:T(8,128)S(1)}, f32[8,512,128]{1,2,0:T(8,128)}, u32[]{:S(2)}) copy-start(f32[8,512,128]{1,2,0:T(8,128)} %copy.23) | copy-start | bytes 6291460
Sparse Core Ops, SparseCore 0:
  11.2 55.4 all-gather.2

commit v3 on v2

--- a/solution.py
+++ b/solution.py
@@ -34,9 +34,9 @@
 def fold(x, op):
     return op(x.reshape(x.shape[0] // 8, 8, x.shape[1]), axis=0)
 
-def attn_kernel(idx_ref, kv_hbm, q_ref, qT_ref, do_ref, doT_ref,
-                dq_ref, tile_ref, kg_ref,
-                kb, vb, kT, vT, S, E, dk, dv, oT, dqT, mrow, drow, qs, dos, sem):
+def attn_kernel(idx_ref, kv_hbm, x_ref, q_ref, qT_ref, do_ref, doT_ref, qg_ref,
+                dq_ref, tile_ref, kg_ref, gq_ref,
+                kb, vb, kT, vT, S, E, dk, dv, oT, dqT, mrow, drow, qs, dos, dq32, sem):
     H = q_ref.shape[0]
     J = 9
     me = lax.axis_index("ctx")
@@ -50,12 +50,9 @@
     for a, b in cps:
         a.wait(); b.wait()
 
-    @pl.loop(0, J)
-    def _(j):
-        kT[j] = kb[j].T
-        vT[j] = vb[j].T
-        dk[j] = jnp.zeros(dk.shape[1:], F32)
-        dv[j] = jnp.zeros(dv.shape[1:], F32)
+    kg_ref[...] = jnp.zeros(kg_ref.shape, F32)
+    gq_ref[...] = jnp.zeros(gq_ref.shape, F32)
+    tile_ref[J] = jnp.zeros(tile_ref.shape[1:], BF)
 
     rows = lax.broadcasted_iota(jnp.int32, (512, 512), 0)
     cols = lax.broadcasted_iota(jnp.int32, (512, 512), 1)
@@ -64,7 +61,7 @@
         s = dot(kb[j], qT_ref[h])
         if own:
             s = jnp.where(rows <= cols, s, NEG)
-        S[h % 2, j] = s
+        S[j] = s
         cm = fold(s, jnp.max)
         if not own:
             cm = jnp.where(idx_ref[j] >= 0, cm, NEG)
@@ -74,11 +71,11 @@
         m = mrow[h % 2]
         if not own:
             m = jnp.where(idx_ref[j] >= 0, m, 1e30)
-        s = S[h % 2, j]
+        s = S[j]
         e = jnp.exp2((s.reshape(64, 8, 512) - m[None]) * C2)
         l = jnp.sum(e, axis=0)
         eb = e.reshape(512, 512).astype(BF)
-        E[h % 2, j] = eb
+        E[j] = eb
         oT[...] += dot(vT[j], eb)
         return l
 
@@ -86,7 +83,7 @@
         dp = dot(vb[j], doT_ref[h])
         dl = drow[h % 2]
         dpb = (dp.reshape(64, 8, 512) - dl[None]).reshape(512, 512).astype(BF)
-        eb = E[h % 2, j]
+        eb = E[j]
         ds = eb * dpb
         dv[j] += dot(eb, dos[h % 2])
         dk[j] += dot(ds, qs[h % 2])
@@ -100,20 +97,35 @@
 
         def body(j, carry, own=False):
             mx, l = carry
+            if a1 and not a2:
+                vT[j] = vb[j].T
+            if a1 and a2 and not c:
+                kT[j] = kb[j].T
+                dk[j] = jnp.zeros(dk.shape[1:], F32)
+                dv[j] = jnp.zeros(dv.shape[1:], F32)
+            if c:
+                C(t - 2, j)
+            if a2:
+                l = l + A2(t - 1, j, own)
             if a1:
                 mx = jnp.maximum(mx, A1(t, j, own))
-            if a2:
-                l = l + A2(t - 1, j, own)
-            if c:
-                C(t - 2, j)
+            if c and not a2:
+                kg_ref[...] += fold(dk[j] * kb[j].astype(F32), jnp.sum)
+                tile_ref[j, :, 0:128] = dk[j].astype(BF)
+                tile_ref[j, :, 128:256] = dv[j].astype(BF)
             return mx, l
         carry = (jnp.full((8, 512), NEG, F32), jnp.zeros((8, 512), F32))
-        carry = lax.fori_loop(0, J - 1, body, carry)
+        carry = lax.fori_loop(0, J - 1, body, carry, unroll=4)
         mx, l = body(J - 1, carry, True)
         if c:
             h = t - 2
             rl = drow[h % 2 + 2]
-            dq_ref[h] = (dqT[...] * (rl[:1] * SC)).T
+            dq = (dqT[...] * (rl[:1] * SC)).T
+            x = x_ref[h].astype(F32)
+            rq = lax.rsqrt(jnp.mean(x * x, axis=1, keepdims=True) + EPS)
+            dq_raw, gq = norm_back(x, rq, qg_ref[...], dq)
+            dq32[pl.ds(h, 512, stride=8), :] = dq_raw
+            gq_ref[...] += fold(gq, jnp.sum)
         if a2:
             h = t - 1
             l1 = jnp.sum(l, axis=0, keepdims=True)
@@ -138,14 +150,7 @@
     step(H, False, True, True)
     step(H + 1, False, False, True)
 
-    kg_ref[...] = jnp.zeros(kg_ref.shape, F32)
-    tile_ref[J] = jnp.zeros(tile_ref.shape[1:], BF)
-
-    @pl.loop(0, J)
-    def _(j):
-        kg_ref[...] += fold(dk[j] * kb[j].astype(F32), jnp.sum)
-        tile_ref[j, :, 0:128] = dk[j].astype(BF)
-        tile_ref[j, :, 128:256] = dv[j].astype(BF)
+    dq_ref[...] = dq32[...].astype(BF)
 
 
 MESH = pl.DeviceIdType.MESH
@@ -325,30 +330,32 @@
     )(slot, tile, g)
 
 
-def attn(idx, kv_all, q, qT, do, doT):
+def attn(idx, kv_all, x, q, qT, do, doT, qg):
     H = q.shape[0]
     V = functools.partial(pl.BlockSpec, memory_space=pltpu.VMEM)
     return pl.pallas_call(
         attn_kernel,
         out_shape=(
-            jax.ShapeDtypeStruct((H, 512, 128), F32),
+            jax.ShapeDtypeStruct((512 * H, 128), BF),
             jax.ShapeDtypeStruct((10, 512, 256), BF),
             jax.ShapeDtypeStruct((8, 128), F32),
+            jax.ShapeDtypeStruct((8, 128), F32),
         ),
-        in_specs=[pl.BlockSpec(memory_space=pltpu.SMEM), pl.BlockSpec(memory_space=pl.ANY), V(), V(), V(), V()],
-        out_specs=(V(), V(), V()),
+        in_specs=[pl.BlockSpec(memory_space=pltpu.SMEM), pl.BlockSpec(memory_space=pl.ANY), V(), V(), V(), V(), V(), V()],
+        out_specs=(V(), V(), V(), V()),
         scratch_shapes=[
             pltpu.VMEM((9, 512, 128), BF), pltpu.VMEM((9, 512, 128), BF),
             pltpu.VMEM((9, 128, 512), BF), pltpu.VMEM((9, 128, 512), BF),
-            pltpu.VMEM((2, 9, 512, 512), F32), pltpu.VMEM((2, 9, 512, 512), BF),
+            pltpu.VMEM((9, 512, 512), F32), pltpu.VMEM((9, 512, 512), BF),
             pltpu.VMEM((9, 512, 128), F32), pltpu.VMEM((9, 512, 128), F32),
             pltpu.VMEM((128, 512), F32), pltpu.VMEM((128, 512), F32),
             pltpu.VMEM((2, 8, 512), F32), pltpu.VMEM((4, 8, 512), F32),
             pltpu.VMEM((2, 512, 128), BF), pltpu.VMEM((2, 512, 128), BF),
+            pltpu.VMEM((512 * H, 128), F32),
             pltpu.SemaphoreType.DMA((2, 9)),
         ],
         compiler_params=pltpu.CompilerParams(vmem_limit_bytes=60 * 2 ** 20),
-    )(idx, kv_all, q, qT, do, doT)
+    )(idx, kv_all, x, q, qT, do, doT, qg)
 
 
 def on_device(q_raw, k_raw, values, dout, q_gain, k_gain, chosen):
@@ -357,12 +364,13 @@
     k2, v2 = k_raw.reshape(blk, width), values.reshape(blk, width)
     xk, rk, kn = norm_fwd(k2, k_gain)
     kv_all = lax.all_gather(jnp.concatenate([kn, v2], axis=1), "ctx", axis=0)
-    xq, rq, qn = norm_fwd(jnp.transpose(q_raw, (1, 0, 2)), q_gain)
+    xq = jnp.transpose(q_raw, (1, 0, 2))
+    _, _, qn = norm_fwd(xq, q_gain)
     do = jnp.transpose(dout, (1, 0, 2))
     idx = chosen.reshape(-1)
-    dq, tile, kg = attn(idx, kv_all, qn, jnp.swapaxes(qn, 1, 2), do, jnp.swapaxes(do, 1, 2))
-    dq_raw, gq = norm_back(xq, rq, q_gain, dq)
-    part_q = jnp.sum(gq.reshape(-1, width), axis=0)
+    dq_raw, tile, kg, gq = attn(
+        idx, kv_all, xq, qn, jnp.swapaxes(qn, 1, 2), do, jnp.swapaxes(do, 1, 2), q_gain[None])
+    part_q = jnp.sum(gq, axis=0)
     part_k = jnp.sum(kg, axis=0) / k_gain
     target = jnp.concatenate([idx, position[None]])
     match = target[None, :] == jnp.arange(32, dtype=jnp.int32)[:, None]
@@ -371,7 +379,7 @@
     dkn, dvalues, gains = scatter(slot, tile, parts)
     dk_raw, _ = norm_back(xk, rk, k_gain, dkn)
     return (
-        jnp.transpose(dq_raw.astype(BF), (1, 0, 2)),
+        dq_raw.reshape(blk, heads, width),
         dk_raw.astype(BF).reshape(blk, 1, width),
         dvalues.reshape(blk, 1, width),
         gains[0],

time: 211 us -> 182 us (0.86)
  Pallas kernels: 127 us -> 102 us
  local copies, waits for them, and re-layouts: 11.6 us -> 7.98 us
    pallas_call x1, Pallas kernels: 91.3 us -> 67.1 us  [attn(): pl.pallas_call(attn_kernel, out_shape=(jax.ShapeDtypeStruct((512 * H, 128...]
    pallas_call x1 -> x0, local copies, waits for them, and re-layouts: 2.95 us -> none  [attn(): pl.pallas_call(attn_kernel, out_shape=(jax.ShapeDtypeStruct((H, 512, 128)...]
    reduce_sum x1, other arithmetic: 2.94 us -> 0.7 us  [on_device(): part_q = jnp.sum(gq, axis=0)]
    unnamed x27 -> x17, local copies, waits for them, and re-layouts: 6.78 us -> 5.66 us
  transfers between devices with their start and end apart: 1 -> 1, of which waited for: 1 -> 1; matrix products, arithmetic and copies ran while one was open for 4% -> 5% of each run, Pallas kernels for 0% -> 0%
where the time goes in v3:
time: 182 us; the launch traced here: 181 us
  Pallas kernels  102 us (56%)
  waiting for transfers between devices  46.9 us (26%)
  between operations  14.2 us (8%)
  other arithmetic  9.96 us (5%)
  local copies, waits for them, and re-layouts  7.98 us (4%)
    pallas_call x1, Pallas kernels, attn(): pl.pallas_call(attn_kernel, out_shape=(jax.ShapeDtypeStruct((512 * H, 128...  67.1 us
    all_gather x1, waiting for transfers between devices, on_device(): kv_all = lax.all_gather(jnp.concatenate([kn, v2], axis=1), 'ctx', axis=0)  46.9 us
    pallas_call x1, Pallas kernels, scatter(): pl.pallas_call(scatter_kernel, out_shape=(jax.ShapeDtypeStruct((512, 128)...  35.4 us
    unnamed x17, local copies, waits for them, and re-layouts  5.66 us
    convert_element_type x3, other arithmetic, norm_fwd(): return (x, scale_r, (x * scale_r * gain).astype(jnp.bfloat16))  3.88 us
  transfers between devices with their start and end apart: 1, of which 1 were waited for; matrix products, arithmetic and copies ran while one was open for 5% of the time, Pallas kernels for 0%

profile of v3, /device:TPU:0, one launch (start us, length us, event | category | flops | bytes accessed | tf_op | source)
XLA Modules:
  0.0 181.5 jit_solution(16631666746864877061)
XLA Ops:
  7.2 0.0 all-gather.3.cloned.1.call-start
  7.2 1.1 fusion.12
  8.4 1.0 fusion.7
  9.4 1.6 pad_maximum_fusion
  11.1 1.7 copy.17
  12.9 1.5 copy.19
  14.4 0.1 pad.2.clone
  14.5 0.1 pad_add_fusion
  14.5 0.1 select_reduce_fusion.slot_ref
  14.6 0.6 fusion
  15.3 1.5 fusion.2.q_ref
  16.8 1.3 fusion.4.qT_ref
  18.1 1.7 copy_bitcast_fusion
  19.8 46.9 %all-gather.3.cloned.1.call-done = bf16[16384,256]{1,0:T(8,128)(2,1)} async-done(((bf16[512,256]{1,0:T(8,128)(2,1)}), bf16[16384,256]{1,0:T(8,128)(2,1)}) %all-gather.3.cloned.1.call-update) | async-done | bytes 8388624 | tf_op jit(solution)/shard_map/all_gather | solution.py:366
  66.7 67.1 %shard_map.110 = (bf16[4096,128]{1,0:T(8,128)(2,1)}, bf16[10,512,256]{2,1,0:T(8,128)(2,1)}, f32[8,128]{1,0:T(8,128)}, f32[8,128]{1,0:T(8,128)}) custom-call(s32[8]{0:T(128)} %bitcast.43, bf16[32,512,256]{2,1,0:T(8,128)(2,1)} %bitcast.38, bf16[8,512,128]{2,1,0:T(8,128)(2,1)} %get-tuple-element.22.x_ref, bf16[8,512,128]{2,1,0:T(8,128)(2,1)} %fusion.2.q_ref, ...), custom_call_target="tpu_custom_call" | custom-call | tf_op jit(solution)/shard_map/pallas_call | solution.py:336
  133.8 0.7 reduce_sum.48
  134.5 0.7 reduce_sum.47
  135.2 0.1 maximum_maximum_fusion.g_ref
  135.3 1.7 copy-done
  137.1 35.4 %shard_map.111 = (f32[512,128]{1,0:T(8,128)S(1)}, bf16[512,128]{1,0:T(8,128)(2,1)S(1)}, f32[8,128]{1,0:T(8,128)S(1)}) custom-call(s32[32]{0:T(128)S(1)} %select_reduce_fusion.slot_ref, bf16[10,512,256]{2,1,0:T(8,128)(2,1)S(1)} %copy-done, f32[8,128]{1,0:T(8,128)S(1)} %maximum_maximum_fusion.g_ref), custom_call_target="tpu_custom_call" | custom-call | tf_op jit(solution)/shard_map/pallas_call | solution.py:316
  172.4 0.2 fusion.13
  172.6 0.9 fusion.14
  173.5 0.5 slice_bitcast_fusion
  174.0 0.7 copy.27
  (19 shorter events, 0.1 us)
Async XLA Ops:
  7.2 5.7 %copy-start.2 = (bf16[512,8,128]{2,1,0:T(8,128)(2,1)S(1)}, bf16[512,8,128]{2,1,0:T(8,128)(2,1)}, u32[]{:S(2)}) copy-start(bf16[512,8,128]{2,1,0:T(8,128)(2,1)} %param.10) | copy-start | bytes 3145732
  7.2 59.5 %all-gather.3.cloned.1.call-start = ((), (), s32[]{:S(2)}) async-start(), calls=%async_computation | async-start | bytes 8650752 | tf_op jit(solution)/shard_map/all_gather | solution.py:366
  11.1 3.4 %copy-start.6 = (s32[1,1,8]{2,1,0:T(1,128)S(1)}, s32[1,1,8]{2,1,0:T(1,128)}, u32[]{:S(2)}) copy-start(s32[1,1,8]{2,1,0:T(1,128)} %param.13) | copy-start | bytes 100
  11.1 3.5 %copy-start.1 = (bf16[512,8,128]{2,1,0:T(8,128)(2,1)S(1)}, bf16[512,8,128]{2,1,0:T(8,128)(2,1)}, u32[]{:S(2)}) copy-start(bf16[512,8,128]{2,1,0:T(8,128)(2,1)} %param.7) | copy-start | bytes 3145732
  12.8 2.4 %copy-start.4 = (f32[128]{0:T(128)S(1)}, f32[128]{0:T(128)}, u32[]{:S(2)}) copy-start(f32[128]{0:T(128)} %param.11) | copy-start | bytes 1540
  66.7 67.8 %copy-start.5 = (f32[128]{0:T(128)S(1)}, f32[128]{0:T(128)}, u32[]{:S(2)}) copy-start(f32[128]{0:T(128)} %param.12) | copy-start | bytes 1540
  66.7 105.7 %copy-start.3 = (bf16[512,1,128]{2,0,1:T(8,128)(2,1)S(1)}, bf16[512,1,128]{2,0,1:T(8,128)(2,1)}, u32[]{:S(2)}) copy-start(bf16[512,1,128]{2,0,1:T(8,128)(2,1)} %param.8) | copy-start | bytes 393220
  135.3 1.7 copy-start
Sparse Core Ops, SparseCore 0:
  11.2 55.4 all-gather.2

commit v4 on v3

--- a/solution.py
+++ b/solution.py
@@ -34,19 +34,27 @@
 def fold(x, op):
     return op(x.reshape(x.shape[0] // 8, 8, x.shape[1]), axis=0)
 
-def attn_kernel(idx_ref, kv_hbm, x_ref, q_ref, qT_ref, do_ref, doT_ref, qg_ref,
-                dq_ref, tile_ref, kg_ref, gq_ref,
-                kb, vb, kT, vT, S, E, dk, dv, oT, dqT, mrow, drow, qs, dos, dq32, sem):
-    H = q_ref.shape[0]
+def attn_kernel(idx_ref, kn_hbm, v_hbm, rows_hbm, cols_hbm, gain_ref,
+                dq_ref, tile_ref, g_ref, rows_ref, cols_ref, kg_ref, gq_ref,
+                kb, vb, kT, vT, S, E, dk, dv, oT, dqT, mrow, drow, qs, dos, dq32, sem, hsem):
+    H = rows_hbm.shape[0]
     J = 9
     me = lax.axis_index("ctx")
     cps = []
     for j in range(J):
         blk = jnp.maximum(idx_ref[j], 0) if j < 8 else me
-        cps.append((pltpu.make_async_copy(kv_hbm.at[blk, :, 0:128], kb.at[j], sem.at[0, j]),
-                    pltpu.make_async_copy(kv_hbm.at[blk, :, 128:256], vb.at[j], sem.at[1, j])))
+        cps.append((pltpu.make_async_copy(kn_hbm.at[blk], kb.at[j], sem.at[0, j]),
+                    pltpu.make_async_copy(v_hbm.at[blk], vb.at[j], sem.at[1, j])))
     for a, b in cps:
         a.start(); b.start()
+
+    def operands(h):
+        return (pltpu.make_async_copy(rows_hbm.at[h], rows_ref.at[h], hsem.at[0, h]),
+                pltpu.make_async_copy(cols_hbm.at[h], cols_ref.at[h], hsem.at[1, h]))
+
+    for h in range(H):
+        for cp in operands(h):
+            cp.start()
     for a, b in cps:
         a.wait(); b.wait()
 
@@ -58,7 +66,7 @@
     cols = lax.broadcasted_iota(jnp.int32, (512, 512), 1)
 
     def A1(h, j, own):
-        s = dot(kb[j], qT_ref[h])
+        s = dot(kb[j], cols_ref[h, 0])
         if own:
             s = jnp.where(rows <= cols, s, NEG)
         S[j] = s
@@ -80,7 +88,7 @@
         return l
 
     def C(h, j):
-        dp = dot(vb[j], doT_ref[h])
+        dp = dot(vb[j], cols_ref[h, 1])
         dl = drow[h % 2]
         dpb = (dp.reshape(64, 8, 512) - dl[None]).reshape(512, 512).astype(BF)
         eb = E[j]
@@ -90,6 +98,9 @@
         dqT[...] += dot(kT[j], ds)
 
     def step(t, a1, a2, c):
+        if a1:
+            for cp in operands(t):
+                cp.wait()
         if a2:
             oT[...] = jnp.zeros(oT.shape, F32)
         if c:
@@ -121,9 +132,9 @@
             h = t - 2
             rl = drow[h % 2 + 2]
             dq = (dqT[...] * (rl[:1] * SC)).T
-            x = x_ref[h].astype(F32)
+            x = rows_ref[h, 0].astype(F32)
             rq = lax.rsqrt(jnp.mean(x * x, axis=1, keepdims=True) + EPS)
-            dq_raw, gq = norm_back(x, rq, qg_ref[...], dq)
+            dq_raw, gq = norm_back(x, rq, gain_ref[0:1], dq)
             dq32[pl.ds(h, 512, stride=8), :] = dq_raw
             gq_ref[...] += fold(gq, jnp.sum)
         if a2:
@@ -131,12 +142,12 @@
             l1 = jnp.sum(l, axis=0, keepdims=True)
             rl = jnp.broadcast_to(1.0 / l1, (8, 512))
             o = oT[...]
-            dl = jnp.sum(o * doT_ref[h].astype(F32), axis=0, keepdims=True) * rl[:1]
+            dl = jnp.sum(o * cols_ref[h, 1].astype(F32), axis=0, keepdims=True) * rl[:1]
             drow[h % 2] = jnp.broadcast_to(dl, (8, 512))
             drow[h % 2 + 2] = rl
             rc = rl.T[:, :1]
-            dos[h % 2] = (do_ref[h].astype(F32) * rc).astype(BF)
-            qs[h % 2] = (q_ref[h].astype(F32) * (rc * SC)).astype(BF)
+            dos[h % 2] = (rows_ref[h, 2].astype(F32) * rc).astype(BF)
+            qs[h % 2] = (rows_ref[h, 1].astype(F32) * (rc * SC)).astype(BF)
         if a1:
             m = jnp.max(mx, axis=0, keepdims=True)
             mrow[t % 2] = jnp.broadcast_to(m, (8, 512))
@@ -151,6 +162,10 @@
     step(H + 1, False, False, True)
 
     dq_ref[...] = dq32[...].astype(BF)
+    part_q = jnp.sum(gq_ref[...], axis=0, keepdims=True)
+    part_k = jnp.sum(kg_ref[...], axis=0, keepdims=True) / gain_ref[1:2]
+    row = lax.broadcasted_iota(jnp.int32, (8, 128), 0)
+    g_ref[...] = jnp.where(row == 0, part_q, jnp.where(row == 1, part_k, 0.0))
 
 
 MESH = pl.DeviceIdType.MESH
@@ -172,8 +187,8 @@
     pl.semaphore_wait(barrier, len(devices))
 
 
-def scatter_kernel(slot_ref, tile_ref, g_ref, dk_ref, dv_ref, gout_ref,
-                   A, B, cur, R1, R2, T, Q1, Q2, GS, GZ, GX, GY,
+def scatter_kernel(slot_ref, tile_hbm, g_ref, dk_ref, dv_ref, gout_ref,
+                   tile_ref, tsem, A, B, cur, R1, R2, T, Q1, Q2, GS, GZ, GX, GY,
                    s0, r0, s1, r1, s2, r2, sg, rg):
     z, x, c, y = place()
 
@@ -184,6 +199,8 @@
             return peer(z, (x + off) % 4, c, y)
         return peer(z, x, c, (y + off) % 4)
 
+    fetch = pltpu.make_async_copy(tile_hbm, tile_ref, tsem)
+    fetch.start()
     sib = peer(z, x, 1 - c, y)
     greet([sib] + [along(a, o) for a in "zxy" for o in (1, 2, 3)])
     pending = []
@@ -195,6 +212,7 @@
         pending.append(cp)
         return cp
 
+    fetch.wait()
     gcp = send(g_ref, GS, sg.at[0], rg.at[0], sib)
 
     axes = (("z", "x"), ("x", "z"))
@@ -317,33 +335,173 @@
         scatter_kernel,
         out_shape=(jax.ShapeDtypeStruct((512, 128), F32), jax.ShapeDtypeStruct((512, 128), BF),
                    jax.ShapeDtypeStruct((8, 128), F32)),
-        in_specs=[pl.BlockSpec(memory_space=pltpu.SMEM), V(), V()],
+        in_specs=[pl.BlockSpec(memory_space=pltpu.SMEM), pl.BlockSpec(memory_space=pl.ANY), V()],
         out_specs=(V(), V(), V()),
         scratch_shapes=[
+            pltpu.VMEM((10, 512, 256), BF), D(()),
             pltpu.VMEM((2, 4, 4, 512, 128), BF), pltpu.VMEM((2, 4, 4, 512, 128), BF), pltpu.VMEM((2, 4, 4, 512, 128), BF),
             pltpu.VMEM((2, 2, 2, 512, 128), BF), pltpu.VMEM((2, 2, 4, 512, 128), BF),
             pltpu.VMEM((2, 4, 512, 128), BF), pltpu.VMEM((2, 2, 256, 128), BF), pltpu.VMEM((2, 2, 512, 128), BF),
             pltpu.VMEM((8, 128), F32), pltpu.VMEM((4, 8, 128), F32), pltpu.VMEM((4, 8, 128), F32), pltpu.VMEM((4, 8, 128), F32),
             D((8,)), D((8,)), D((2, 6)), D((2, 6)), D((2, 6)), D((2, 6)), D((10,)), D((10,)),
         ],
-        compiler_params=pltpu.CompilerParams(collective_id=1, has_side_effects=True, vmem_limit_bytes=48 * 2 ** 20),
+        compiler_params=pltpu.CompilerParams(collective_id=1, has_side_effects=True, vmem_limit_bytes=60 * 2 ** 20),
     )(slot, tile, g)
 
 
-def attn(idx, kv_all, x, q, qT, do, doT, qg):
-    H = q.shape[0]
+def gather_kernel(k_ref, v_ref, q_ref, do_ref, gain_ref, ko_ref, vo_ref, rows_out, cols_out,
+                  kn_ref, q32, do32, rows, cols, lsem, psem, ss, rs):
+    z, x, c, y = place()
+
+    def along(axis, off):
+        return peer((z + off) % 4, x, c, y) if axis == "z" else peer(z, (x + off) % 4, c, y)
+
+    _, _, kn = norm_fwd(k_ref[...], gain_ref[1:2])
+    kn_ref[...] = kn
+    sib = peer(z, x, 1 - c, y)
+    greet([sib] + [along(a, o) for a in "zx" for o in (1, 3)])
+    coord = {"z": z, "x": x}
+    pending = []
+    sibling = []
+    count = [0, 0]
+
+    halves = ((kn_ref, ko_ref, "x", "z"), (v_ref, vo_ref, "z", "x"))
+    lo, hi, full = slice(0, 256), slice(256, 512), slice(0, 512)
+
+    def block(half, uo, wo, cc=None):
+        cc = c if cc is None else cc
+        u = (coord[halves[half][2]] + uo) % 4
+        w = (coord[halves[half][3]] + wo) % 4
+        return u * 2 + w * 8 + cc if half == 0 else u * 8 + w * 2 + cc
+
+    def send(half, uo, wo, rows, to, src=None):
+        out = halves[half][1]
+        k = count[half]
+        count[half] += 1
+        b = block(half, uo, wo)
+        cp = pltpu.make_async_remote_copy(
+            src_ref=out.at[b, rows] if src is None else src, dst_ref=out.at[b, rows],
+            send_sem=ss.at[half, k], recv_sem=rs.at[half, k], device_id=to, device_id_type=MESH)
+        cp.start()
+        pending.append(cp)
+        return cp
+
+    local = []
+    for half, (src, out, u, w) in enumerate(halves):
+        cp = pltpu.make_async_copy(src, out.at[block(half, 0, 0)], lsem.at[half])
+        cp.start()
+        local.append(cp)
+    got = {}
+    for half, (src, out, u, w) in enumerate(halves):
+        got[half, "u+"] = send(half, 0, 0, full, along(u, 1), src)
+        got[half, "u-"] = send(half, 0, 0, full, along(u, 3), src)
+    q32[...] = q_ref[...].astype(F32)
+    do32[...] = do_ref[...].astype(F32)
+
+    def prep(h):
+        x = q32[pl.ds(h, 512, stride=8), :]
+        _, _, qn = norm_fwd(x, gain_ref[0:1])
+        d = do32[pl.ds(h, 512, stride=8), :].astype(BF)
+        rows[h, 0] = x.astype(BF)
+        rows[h, 1] = qn
+        rows[h, 2] = d
+        cols[h, 0] = qn.T
+        cols[h, 1] = d.T
+        for n, (src, dst) in enumerate(((rows, rows_out), (cols, cols_out))):
+            cp = pltpu.make_async_copy(src.at[h], dst.at[h], psem.at[n, h])
+            cp.start()
+            local.append(cp)
+
+    for half, (src, out, u, w) in enumerate(halves):
+        got[half, 0, "w+"] = send(half, 0, 0, full, along(w, 1), src)
+        got[half, 0, "w-"] = send(half, 0, 0, full, along(w, 3), src)
+        sibling.append(send(half, 0, 0, full, sib, src))
+    prep(0)
+    for half, (src, out, u, w) in enumerate(halves):
+        got[half, "u+"].wait_recv()
+        got[half, "f+"] = send(half, 3, 0, lo, along(u, 1))
+        got[half, 3, "w+"] = send(half, 3, 0, full, along(w, 1))
+        got[half, 3, "w-"] = send(half, 3, 0, full, along(w, 3))
+        sibling.append(send(half, 3, 0, full, sib))
+        got[half, "u-"].wait_recv()
+        got[half, "f-"] = send(half, 1, 0, hi, along(u, 3))
+        got[half, 1, "w+"] = send(half, 1, 0, full, along(w, 1))
+        got[half, 1, "w-"] = send(half, 1, 0, full, along(w, 3))
+        sibling.append(send(half, 1, 0, full, sib))
+
+    def onward(half, uo):
+        w = halves[half][3]
+        got[half, uo, "w+"].wait_recv()
+        got[half, uo, "g+"] = send(half, uo, 3, lo, along(w, 1))
+        sibling.append(send(half, uo, 3, full, sib))
+        got[half, uo, "w-"].wait_recv()
+        got[half, uo, "g-"] = send(half, uo, 1, hi, along(w, 3))
+        sibling.append(send(half, uo, 1, full, sib))
+
+    prep(1)
+    for half in (0, 1):
+        onward(half, 0)
+    prep(2)
+    for half, (src, out, u, w) in enumerate(halves):
+        got[half, "f+"].wait_recv()
+        got[half, "f-"].wait_recv()
+        got[half, 2, "w+"] = send(half, 2, 0, full, along(w, 1))
+        got[half, 2, "w-"] = send(half, 2, 0, full, along(w, 3))
+        sibling.append(send(half, 2, 0, full, sib))
+    for uo in (3, 1, 2):
+        prep(3 + (uo % 3))
+        for half in (0, 1):
+            onward(half, uo)
+    prep(6)
+    prep(7)
+    for uo in (0, 3, 1, 2):
+        for half in (0, 1):
+            got[half, uo, "g+"].wait_recv()
+            got[half, uo, "g-"].wait_recv()
+            sibling.append(send(half, uo, 2, full, sib))
+    for cp in sibling:
+        cp.wait_recv()
+    for cp in pending:
+        cp.wait_send()
+    for cp in local:
+        cp.wait()
+
+
+def gather(k, v, q, do, gains):
+    D = pltpu.SemaphoreType.DMA
+    anys = pl.BlockSpec(memory_space=pl.ANY)
+    vm = pl.BlockSpec(memory_space=pltpu.VMEM)
+    return pl.pallas_call(
+        gather_kernel,
+        out_shape=(jax.ShapeDtypeStruct((32, 512, 128), BF), jax.ShapeDtypeStruct((32, 512, 128), BF),
+                   jax.ShapeDtypeStruct((8, 3, 512, 128), BF), jax.ShapeDtypeStruct((8, 2, 128, 512), BF)),
+        in_specs=[vm] * 5,
+        out_specs=(anys,) * 4,
+        scratch_shapes=[
+            pltpu.VMEM((512, 128), BF), pltpu.VMEM((4096, 128), F32), pltpu.VMEM((4096, 128), F32),
+            pltpu.VMEM((8, 3, 512, 128), BF), pltpu.VMEM((8, 2, 128, 512), BF),
+            D((2,)), D((2, 8)), D((2, 36)), D((2, 36)),
+        ],
+        compiler_params=pltpu.CompilerParams(collective_id=0, has_side_effects=True, vmem_limit_bytes=60 * 2 ** 20),
+    )(k, v, q, do, gains)
+
+
+def attn(idx, kn_all, v_all, rows, cols, gains):
+    H = rows.shape[0]
     V = functools.partial(pl.BlockSpec, memory_space=pltpu.VMEM)
+    A = functools.partial(pl.BlockSpec, memory_space=pl.ANY)
     return pl.pallas_call(
         attn_kernel,
         out_shape=(
             jax.ShapeDtypeStruct((512 * H, 128), BF),
             jax.ShapeDtypeStruct((10, 512, 256), BF),
             jax.ShapeDtypeStruct((8, 128), F32),
-            jax.ShapeDtypeStruct((8, 128), F32),
         ),
-        in_specs=[pl.BlockSpec(memory_space=pltpu.SMEM), pl.BlockSpec(memory_space=pl.ANY), V(), V(), V(), V(), V(), V()],
-        out_specs=(V(), V(), V(), V()),
+        in_specs=[pl.BlockSpec(memory_space=pltpu.SMEM), A(), A(), A(), A(), V()],
+        out_specs=(V(), V(), V()),
         scratch_shapes=[
+            pltpu.VMEM((H, 3, 512, 128), BF), pltpu.VMEM((H, 2, 128, 512), BF),
+            pltpu.VMEM((8, 128), F32), pltpu.VMEM((8, 128), F32),
             pltpu.VMEM((9, 512, 128), BF), pltpu.VMEM((9, 512, 128), BF),
             pltpu.VMEM((9, 128, 512), BF), pltpu.VMEM((9, 128, 512), BF),
             pltpu.VMEM((9, 512, 512), F32), pltpu.VMEM((9, 512, 512), BF),
@@ -352,38 +510,33 @@
             pltpu.VMEM((2, 8, 512), F32), pltpu.VMEM((4, 8, 512), F32),
             pltpu.VMEM((2, 512, 128), BF), pltpu.VMEM((2, 512, 128), BF),
             pltpu.VMEM((512 * H, 128), F32),
-            pltpu.SemaphoreType.DMA((2, 9)),
+            pltpu.SemaphoreType.DMA((2, 9)), pltpu.SemaphoreType.DMA((2, H)),
         ],
         compiler_params=pltpu.CompilerParams(vmem_limit_bytes=60 * 2 ** 20),
-    )(idx, kv_all, x, q, qT, do, doT, qg)
+    )(idx, kn_all, v_all, rows, cols, gains)
 
 
 def on_device(q_raw, k_raw, values, dout, q_gain, k_gain, chosen):
     blk, heads, width = q_raw.shape
     position = lax.axis_index("ctx")
     k2, v2 = k_raw.reshape(blk, width), values.reshape(blk, width)
-    xk, rk, kn = norm_fwd(k2, k_gain)
-    kv_all = lax.all_gather(jnp.concatenate([kn, v2], axis=1), "ctx", axis=0)
-    xq = jnp.transpose(q_raw, (1, 0, 2))
-    _, _, qn = norm_fwd(xq, q_gain)
-    do = jnp.transpose(dout, (1, 0, 2))
+    gains = jnp.concatenate([q_gain[None], k_gain[None], jnp.ones((6, width), F32)], axis=0)
+    kn_all, v_all, rows, cols = gather(
+        k2, v2, q_raw.reshape(blk * heads, width), dout.reshape(blk * heads, width), gains)
     idx = chosen.reshape(-1)
-    dq_raw, tile, kg, gq = attn(
-        idx, kv_all, xq, qn, jnp.swapaxes(qn, 1, 2), do, jnp.swapaxes(do, 1, 2), q_gain[None])
-    part_q = jnp.sum(gq, axis=0)
-    part_k = jnp.sum(kg, axis=0) / k_gain
+    dq_raw, tile, parts = attn(idx, kn_all, v_all, rows, cols, gains)
     target = jnp.concatenate([idx, position[None]])
     match = target[None, :] == jnp.arange(32, dtype=jnp.int32)[:, None]
     slot = jnp.min(jnp.where(match, jnp.arange(9, dtype=jnp.int32)[None, :], 9), axis=1)
-    parts = jnp.concatenate([part_q[None], part_k[None], jnp.zeros((6, width), F32)], axis=0)
-    dkn, dvalues, gains = scatter(slot, tile, parts)
+    dkn, dvalues, sums = scatter(slot, tile, parts)
+    xk, rk, _ = norm_fwd(k2, k_gain)
     dk_raw, _ = norm_back(xk, rk, k_gain, dkn)
     return (
         dq_raw.reshape(blk, heads, width),
         dk_raw.astype(BF).reshape(blk, 1, width),
         dvalues.reshape(blk, 1, width),
-        gains[0],
-        gains[1],
+        sums[0],
+        sums[1],
     )
 
 

time: 182 us -> 148 us (0.81)
  waiting for transfers between devices: 46.9 us -> 0 us
  Pallas kernels: 102 us -> 139 us
  between operations: 14.2 us -> 0.73 us
  local copies, waits for them, and re-layouts: 7.98 us -> 2.93 us
  other arithmetic: 9.96 us -> 4.99 us
    all_gather x1 -> x0, waiting for transfers between devices: 46.9 us -> none  [on_device(): kv_all = lax.all_gather(jnp.concatenate([kn, v2], axis=1), 'ctx', axis=0)]
    pallas_call x0 -> x1, Pallas kernels: none -> 33.9 us  [gather(): pl.pallas_call(gather_kernel, out_shape=(jax.ShapeDtypeStruct((32, 512, 1...]
    unnamed x17 -> x7, local copies, waits for them, and re-layouts: 5.66 us -> 1.59 us
    convert_element_type x3 -> x0, other arithmetic: 3.88 us -> none  [norm_fwd(): return (x, scale_r, (x * scale_r * gain).astype(jnp.bfloat16))]
  transfers between devices with their start and end apart: 1 -> 0, of which waited for: 1 -> 0; matrix products, arithmetic and copies ran while one was open for 5% -> 0% of each run, Pallas kernels for 0% -> 0%
where the time goes in v4:
time: 148 us
  Pallas kernels  139 us (94%)
  other arithmetic  4.99 us (3%)
  local copies, waits for them, and re-layouts  2.93 us (2%)
    pallas_call x1, Pallas kernels, attn(): pl.pallas_call(attn_kernel, out_shape=(jax.ShapeDtypeStruct((512 * H, 128...  68.5 us
    pallas_call x1, Pallas kernels, scatter(): pl.pallas_call(scatter_kernel, out_shape=(jax.ShapeDtypeStruct((512, 128)...  36.6 us
    pallas_call x1, Pallas kernels, gather(): pl.pallas_call(gather_kernel, out_shape=(jax.ShapeDtypeStruct((32, 512, 1...  33.9 us

profile of v4, /device:TPU:0, one launch (start us, length us, event | category | flops | bytes accessed | tf_op | source)
XLA Modules:
  0.0 147.7 jit_solution(6991770264116432767)
XLA Ops:
  0.6 0.1 pad.4.clone
  0.7 1.3 maximum_maximum_fusion.gain_ref
  2.0 33.9 %shard_map.110 = (bf16[32,512,128]{2,1,0:T(8,128)(2,1)}, bf16[32,512,128]{2,1,0:T(8,128)(2,1)}, bf16[8,3,512,128]{3,2,1,0:T(8,128)(2,1)}, bf16[8,2,128,512]{3,2,1,0:T(8,128)(2,1)}) custom-call(bf16[512,128]{1,0:T(8,128)(2,1)} %bitcast.19, bf16[512,128]{1,0:T(8,128)(2,1)} %bitcast.22, bf16[4096,128]{1,0:T(8,128)(2,1)} %bitcast.20, ...), custom_call_target="tpu_custom_call" | custom-call | tf_op jit(solution)/shard_map/pallas_call | solution.py:474
  36.0 0.0 copy-start.2
  36.0 0.0 copy-start
  36.0 0.0 copy-start.1
  36.0 68.5 %shard_map.111 = (bf16[4096,128]{1,0:T(8,128)(2,1)}, bf16[10,512,256]{2,1,0:T(8,128)(2,1)}, f32[8,128]{1,0:T(8,128)}) custom-call(s32[8]{0:T(128)} %bitcast.25, bf16[32,512,128]{2,1,0:T(8,128)(2,1)} %get-tuple-element.15.kn_hbm, bf16[32,512,128]{2,1,0:T(8,128)(2,1)} %get-tuple-element.16.v_hbm, bf16[8,3,512,128]{3,2,1,0:T(8,128)(2,1)} %get-tuple-element.17.rows_hbm, ...), custom_call_target="tpu_custom_call" | custom-call | tf_op jit(solution)/shard_map/pallas_call | solution.py:493
  104.5 0.0 copy-done.2
  104.6 0.1 pad_add_fusion
  104.6 0.6 select_reduce_fusion.slot_ref
  105.2 36.6 %shard_map.112 = (f32[512,128]{1,0:T(8,128)}, bf16[512,128]{1,0:T(8,128)(2,1)}, f32[8,128]{1,0:T(8,128)}) custom-call(s32[32]{0:T(128)} %select_reduce_fusion.slot_ref, bf16[10,512,256]{2,1,0:T(8,128)(2,1)} %get-tuple-element.20.tile_hbm, f32[8,128]{1,0:T(8,128)} %get-tuple-element.21.g_ref), custom_call_target="tpu_custom_call" | custom-call | tf_op jit(solution)/shard_map/pallas_call | solution.py:334
  141.8 0.0 copy-done
  141.8 0.0 copy-done.1
  141.9 1.2 fusion
  143.0 1.8 %fusion.7 = bf16[512,1,128]{2,0,1:T(8,128)(2,1)} fusion(f32[512,128]{1,0:T(8,128)} %get-tuple-element.22, f32[512]{0:T(512)S(1)} %get-tuple-element.30, f32[128]{0:T(128)S(1)} %copy-done.1, f32[512]{0:T(512)S(1)} %get-tuple-element.29, bf16[512,1,128]{2,0,1:T(8,128)(2,1)S(1)} %copy-done), kind=kLoop, calls=%fused_computation.10 | loop fusion | flops 524288 | bytes 528896 | tf_op jit(solution)/shard_map/reshape | solution.py:536
  144.9 1.3 slice_bitcast_fusion
  146.1 1.6 %copy.13 = bf16[512,1,128]{2,0,1:T(8,128)(2,1)} copy(bf16[512,1,128]{2,0,1:T(8,128)(2,1)} %bitcast.23) | data formatting | bytes 262144
  (2 shorter events, 0.0 us)
Async XLA Ops:
  36.0 68.6 %copy-start.2 = (s32[1,1,8]{2,1,0:T(1,128)S(1)}, s32[1,1,8]{2,1,0:T(1,128)}, u32[]{:S(2)}) copy-start(s32[1,1,8]{2,1,0:T(1,128)} %param.13) | copy-start | bytes 100
  36.0 105.9 %copy-start = (bf16[512,1,128]{2,0,1:T(8,128)(2,1)S(1)}, bf16[512,1,128]{2,0,1:T(8,128)(2,1)}, u32[]{:S(2)}) copy-start(bf16[512,1,128]{2,0,1:T(8,128)(2,1)} %param.8) | copy-start | bytes 393220
  36.0 105.8 %copy-start.1 = (f32[128]{0:T(128)S(1)}, f32[128]{0:T(128)}, u32[]{:S(2)}) copy-start(f32[128]{0:T(128)} %param.12) | copy-start | bytes 1540

commit v5 on v4

--- a/solution.py
+++ b/solution.py
@@ -34,33 +34,41 @@
 def fold(x, op):
     return op(x.reshape(x.shape[0] // 8, 8, x.shape[1]), axis=0)
 
-def attn_kernel(idx_ref, kn_hbm, v_hbm, rows_hbm, cols_hbm, gain_ref,
-                dq_ref, tile_ref, g_ref, rows_ref, cols_ref, kg_ref, gq_ref,
-                kb, vb, kT, vT, S, E, dk, dv, oT, dqT, mrow, drow, qs, dos, dq32, sem, hsem):
+def attn_kernel(idx_ref, kn_hbm, v_hbm, rows_hbm, cols_hbm, qgain_ref, kgain_ref,
+                dq_ref, tile_hbm, g_ref, slot_ref, tile_ref, rows_ref, cols_ref, kg_ref, gq_ref,
+                kb, vb, kT, S, DP, E, dk, dv, dqT, mrow, drow, qs, dos, dq32, sem, hsem):
     H = rows_hbm.shape[0]
     J = 9
     me = lax.axis_index("ctx")
-    cps = []
-    for j in range(J):
-        blk = jnp.maximum(idx_ref[j], 0) if j < 8 else me
-        cps.append((pltpu.make_async_copy(kn_hbm.at[blk], kb.at[j], sem.at[0, j]),
-                    pltpu.make_async_copy(v_hbm.at[blk], vb.at[j], sem.at[1, j])))
-    for a, b in cps:
-        a.start(); b.start()
+    def operand(j, own, n):
+        blk = me if own else jnp.maximum(idx_ref[j], 0)
+        src, dst = ((kn_hbm, kb), (v_hbm, vb))[n]
+        return pltpu.make_async_copy(src.at[blk], dst.at[j], sem.at[n, j])
+
+    def tile_out(j):
+        return pltpu.make_async_copy(tile_ref.at[j], tile_hbm.at[j], sem.at[2, j])
 
     def operands(h):
         return (pltpu.make_async_copy(rows_hbm.at[h], rows_ref.at[h], hsem.at[0, h]),
                 pltpu.make_async_copy(cols_hbm.at[h], cols_ref.at[h], hsem.at[1, h]))
 
-    for h in range(H):
+    for cp in operands(0):
+        cp.start()
+    for n in (0, 1):
+        for j in range(J):
+            operand(j, j == J - 1, n).start()
+    for h in range(1, H):
         for cp in operands(h):
             cp.start()
-    for a, b in cps:
-        a.wait(); b.wait()
-
+    for b in range(40):
+        slot_ref[b] = J
+    for j in range(J - 1):
+        slot_ref[jnp.where(idx_ref[j] >= 0, idx_ref[j], 32)] = j
+    slot_ref[me] = J - 1
     kg_ref[...] = jnp.zeros(kg_ref.shape, F32)
     gq_ref[...] = jnp.zeros(gq_ref.shape, F32)
     tile_ref[J] = jnp.zeros(tile_ref.shape[1:], BF)
+    tile_out(J).start()
 
     rows = lax.broadcasted_iota(jnp.int32, (512, 512), 0)
     cols = lax.broadcasted_iota(jnp.int32, (512, 512), 1)
@@ -84,11 +92,12 @@
         l = jnp.sum(e, axis=0)
         eb = e.reshape(512, 512).astype(BF)
         E[j] = eb
-        oT[...] += dot(vT[j], eb)
-        return l
+        dp = dot(vb[j], cols_ref[h, 1])
+        DP[j] = dp
+        return l, fold(e.reshape(512, 512) * dp, jnp.sum)
 
     def C(h, j):
-        dp = dot(vb[j], cols_ref[h, 1])
+        dp = DP[j]
         dl = drow[h % 2]
         dpb = (dp.reshape(64, 8, 512) - dl[None]).reshape(512, 512).astype(BF)
         eb = E[j]
@@ -101,48 +110,48 @@
         if a1:
             for cp in operands(t):
                 cp.wait()
-        if a2:
-            oT[...] = jnp.zeros(oT.shape, F32)
         if c:
             dqT[...] = jnp.zeros(dqT.shape, F32)
 
         def body(j, carry, own=False):
-            mx, l = carry
+            mx, l, dd = carry
             if a1 and not a2:
-                vT[j] = vb[j].T
+                operand(j, own, 0).wait()
             if a1 and a2 and not c:
+                operand(j, own, 1).wait()
                 kT[j] = kb[j].T
                 dk[j] = jnp.zeros(dk.shape[1:], F32)
                 dv[j] = jnp.zeros(dv.shape[1:], F32)
             if c:
                 C(t - 2, j)
             if a2:
-                l = l + A2(t - 1, j, own)
+                l_j, d_j = A2(t - 1, j, own)
+                l, dd = l + l_j, dd + d_j
             if a1:
                 mx = jnp.maximum(mx, A1(t, j, own))
             if c and not a2:
                 kg_ref[...] += fold(dk[j] * kb[j].astype(F32), jnp.sum)
                 tile_ref[j, :, 0:128] = dk[j].astype(BF)
                 tile_ref[j, :, 128:256] = dv[j].astype(BF)
-            return mx, l
-        carry = (jnp.full((8, 512), NEG, F32), jnp.zeros((8, 512), F32))
-        carry = lax.fori_loop(0, J - 1, body, carry, unroll=4)
-        mx, l = body(J - 1, carry, True)
+                tile_out(j).start()
+            return mx, l, dd
+        carry = (jnp.full((8, 512), NEG, F32), jnp.zeros((8, 512), F32), jnp.zeros((8, 512), F32))
+        carry = lax.fori_loop(0, J - 1, body, carry, unroll=8)
+        mx, l, dd = body(J - 1, carry, True)
         if c:
             h = t - 2
             rl = drow[h % 2 + 2]
             dq = (dqT[...] * (rl[:1] * SC)).T
             x = rows_ref[h, 0].astype(F32)
             rq = lax.rsqrt(jnp.mean(x * x, axis=1, keepdims=True) + EPS)
-            dq_raw, gq = norm_back(x, rq, gain_ref[0:1], dq)
+            dq_raw, gq = norm_back(x, rq, qgain_ref[...], dq)
             dq32[pl.ds(h, 512, stride=8), :] = dq_raw
             gq_ref[...] += fold(gq, jnp.sum)
         if a2:
             h = t - 1
             l1 = jnp.sum(l, axis=0, keepdims=True)
             rl = jnp.broadcast_to(1.0 / l1, (8, 512))
-            o = oT[...]
-            dl = jnp.sum(o * cols_ref[h, 1].astype(F32), axis=0, keepdims=True) * rl[:1]
+            dl = jnp.sum(dd, axis=0, keepdims=True) * rl[:1]
             drow[h % 2] = jnp.broadcast_to(dl, (8, 512))
             drow[h % 2 + 2] = rl
             rc = rl.T[:, :1]
@@ -163,9 +172,11 @@
 
     dq_ref[...] = dq32[...].astype(BF)
     part_q = jnp.sum(gq_ref[...], axis=0, keepdims=True)
-    part_k = jnp.sum(kg_ref[...], axis=0, keepdims=True) / gain_ref[1:2]
+    part_k = jnp.sum(kg_ref[...], axis=0, keepdims=True) / kgain_ref[...]
     row = lax.broadcasted_iota(jnp.int32, (8, 128), 0)
     g_ref[...] = jnp.where(row == 0, part_q, jnp.where(row == 1, part_k, 0.0))
+    for j in range(J + 1):
+        tile_out(j).wait()
 
 
 MESH = pl.DeviceIdType.MESH
@@ -345,18 +356,18 @@
             pltpu.VMEM((8, 128), F32), pltpu.VMEM((4, 8, 128), F32), pltpu.VMEM((4, 8, 128), F32), pltpu.VMEM((4, 8, 128), F32),
             D((8,)), D((8,)), D((2, 6)), D((2, 6)), D((2, 6)), D((2, 6)), D((10,)), D((10,)),
         ],
-        compiler_params=pltpu.CompilerParams(collective_id=1, has_side_effects=True, vmem_limit_bytes=60 * 2 ** 20),
+        compiler_params=pltpu.CompilerParams(collective_id=1, has_side_effects=True, vmem_limit_bytes=62 * 2 ** 20),
     )(slot, tile, g)
 
 
-def gather_kernel(k_ref, v_ref, q_ref, do_ref, gain_ref, ko_ref, vo_ref, rows_out, cols_out,
+def gather_kernel(k_ref, v_ref, q_ref, do_ref, qg_ref, kg_ref, ko_ref, vo_ref, rows_out, cols_out,
                   kn_ref, q32, do32, rows, cols, lsem, psem, ss, rs):
     z, x, c, y = place()
 
     def along(axis, off):
         return peer((z + off) % 4, x, c, y) if axis == "z" else peer(z, (x + off) % 4, c, y)
 
-    _, _, kn = norm_fwd(k_ref[...], gain_ref[1:2])
+    _, _, kn = norm_fwd(k_ref[...], kg_ref[...])
     kn_ref[...] = kn
     sib = peer(z, x, 1 - c, y)
     greet([sib] + [along(a, o) for a in "zx" for o in (1, 3)])
@@ -400,7 +411,7 @@
 
     def prep(h):
         x = q32[pl.ds(h, 512, stride=8), :]
-        _, _, qn = norm_fwd(x, gain_ref[0:1])
+        _, _, qn = norm_fwd(x, qg_ref[...])
         d = do32[pl.ds(h, 512, stride=8), :].astype(BF)
         rows[h, 0] = x.astype(BF)
         rows[h, 1] = qn
@@ -467,7 +478,7 @@
         cp.wait()
 
 
-def gather(k, v, q, do, gains):
+def gather(k, v, q, do, qg, kg):
     D = pltpu.SemaphoreType.DMA
     anys = pl.BlockSpec(memory_space=pl.ANY)
     vm = pl.BlockSpec(memory_space=pltpu.VMEM)
@@ -475,7 +486,7 @@
         gather_kernel,
         out_shape=(jax.ShapeDtypeStruct((32, 512, 128), BF), jax.ShapeDtypeStruct((32, 512, 128), BF),
                    jax.ShapeDtypeStruct((8, 3, 512, 128), BF), jax.ShapeDtypeStruct((8, 2, 128, 512), BF)),
-        in_specs=[vm] * 5,
+        in_specs=[vm] * 6,
         out_specs=(anys,) * 4,
         scratch_shapes=[
             pltpu.VMEM((512, 128), BF), pltpu.VMEM((4096, 128), F32), pltpu.VMEM((4096, 128), F32),
@@ -483,10 +494,10 @@
             D((2,)), D((2, 8)), D((2, 36)), D((2, 36)),
         ],
         compiler_params=pltpu.CompilerParams(collective_id=0, has_side_effects=True, vmem_limit_bytes=60 * 2 ** 20),
-    )(k, v, q, do, gains)
-
-
-def attn(idx, kn_all, v_all, rows, cols, gains):
+    )(k, v, q, do, qg, kg)
+
+
+def attn(idx, kn_all, v_all, rows, cols, qg, kg):
     H = rows.shape[0]
     V = functools.partial(pl.BlockSpec, memory_space=pltpu.VMEM)
     A = functools.partial(pl.BlockSpec, memory_space=pl.ANY)
@@ -496,38 +507,35 @@
             jax.ShapeDtypeStruct((512 * H, 128), BF),
             jax.ShapeDtypeStruct((10, 512, 256), BF),
             jax.ShapeDtypeStruct((8, 128), F32),
+            jax.ShapeDtypeStruct((40,), jnp.int32),
         ),
-        in_specs=[pl.BlockSpec(memory_space=pltpu.SMEM), A(), A(), A(), A(), V()],
-        out_specs=(V(), V(), V()),
+        in_specs=[pl.BlockSpec(memory_space=pltpu.SMEM), A(), A(), A(), A(), V(), V()],
+        out_specs=(V(), A(), V(), pl.BlockSpec(memory_space=pltpu.SMEM)),
         scratch_shapes=[
+            pltpu.VMEM((10, 512, 256), BF),
             pltpu.VMEM((H, 3, 512, 128), BF), pltpu.VMEM((H, 2, 128, 512), BF),
             pltpu.VMEM((8, 128), F32), pltpu.VMEM((8, 128), F32),
             pltpu.VMEM((9, 512, 128), BF), pltpu.VMEM((9, 512, 128), BF),
-            pltpu.VMEM((9, 128, 512), BF), pltpu.VMEM((9, 128, 512), BF),
-            pltpu.VMEM((9, 512, 512), F32), pltpu.VMEM((9, 512, 512), BF),
+            pltpu.VMEM((9, 128, 512), BF),
+            pltpu.VMEM((9, 512, 512), F32), pltpu.VMEM((9, 512, 512), F32), pltpu.VMEM((9, 512, 512), BF),
             pltpu.VMEM((9, 512, 128), F32), pltpu.VMEM((9, 512, 128), F32),
-            pltpu.VMEM((128, 512), F32), pltpu.VMEM((128, 512), F32),
+            pltpu.VMEM((128, 512), F32),
             pltpu.VMEM((2, 8, 512), F32), pltpu.VMEM((4, 8, 512), F32),
             pltpu.VMEM((2, 512, 128), BF), pltpu.VMEM((2, 512, 128), BF),
             pltpu.VMEM((512 * H, 128), F32),
-            pltpu.SemaphoreType.DMA((2, 9)), pltpu.SemaphoreType.DMA((2, H)),
+            pltpu.SemaphoreType.DMA((3, 10)), pltpu.SemaphoreType.DMA((2, H)),
         ],
         compiler_params=pltpu.CompilerParams(vmem_limit_bytes=60 * 2 ** 20),
-    )(idx, kn_all, v_all, rows, cols, gains)
+    )(idx, kn_all, v_all, rows, cols, qg, kg)
 
 
 def on_device(q_raw, k_raw, values, dout, q_gain, k_gain, chosen):
     blk, heads, width = q_raw.shape
-    position = lax.axis_index("ctx")
     k2, v2 = k_raw.reshape(blk, width), values.reshape(blk, width)
-    gains = jnp.concatenate([q_gain[None], k_gain[None], jnp.ones((6, width), F32)], axis=0)
+    qg, kg = q_gain[None], k_gain[None]
     kn_all, v_all, rows, cols = gather(
-        k2, v2, q_raw.reshape(blk * heads, width), dout.reshape(blk * heads, width), gains)
-    idx = chosen.reshape(-1)
-    dq_raw, tile, parts = attn(idx, kn_all, v_all, rows, cols, gains)
-    target = jnp.concatenate([idx, position[None]])
-    match = target[None, :] == jnp.arange(32, dtype=jnp.int32)[:, None]
-    slot = jnp.min(jnp.where(match, jnp.arange(9, dtype=jnp.int32)[None, :], 9), axis=1)
+        k2, v2, q_raw.reshape(blk * heads, width), dout.reshape(blk * heads, width), qg, kg)
+    dq_raw, tile, parts, slot = attn(chosen.reshape(-1), kn_all, v_all, rows, cols, qg, kg)
     dkn, dvalues, sums = scatter(slot, tile, parts)
     xk, rk, _ = norm_fwd(k2, k_gain)
     dk_raw, _ = norm_back(xk, rk, k_gain, dkn)

time: 148 us -> 135 us (0.912)
  Pallas kernels: 139 us -> 128 us
  other arithmetic: 4.99 us -> 2.98 us
    pallas_call x1, Pallas kernels: 68.5 us -> 57.2 us  [attn(): pl.pallas_call(attn_kernel, out_shape=(jax.ShapeDtypeStruct((512 * H, 128...]
where the time goes in v5:
time: 135 us
  Pallas kernels  128 us (95%)
  other arithmetic  2.98 us (2%)
  local copies, waits for them, and re-layouts  2.86 us (2%)
    pallas_call x1, Pallas kernels, attn(): pl.pallas_call(attn_kernel, out_shape=(jax.ShapeDtypeStruct((512 * H, 128...  57.2 us
    pallas_call x1, Pallas kernels, scatter(): pl.pallas_call(scatter_kernel, out_shape=(jax.ShapeDtypeStruct((512, 128)...  37.3 us
    pallas_call x1, Pallas kernels, gather(): pl.pallas_call(gather_kernel, out_shape=(jax.ShapeDtypeStruct((32, 512, 1...  34 us

profile of v5, /device:TPU:0, one launch (start us, length us, event | category | flops | bytes accessed | tf_op | source)
XLA Modules:
  0.0 134.9 jit_solution(18277620754112642545)
XLA Ops:
  0.6 34.0 %shard_map.110 = (bf16[32,512,128]{2,1,0:T(8,128)(2,1)}, bf16[32,512,128]{2,1,0:T(8,128)(2,1)}, bf16[8,3,512,128]{3,2,1,0:T(8,128)(2,1)}, bf16[8,2,128,512]{3,2,1,0:T(8,128)(2,1)}) custom-call(bf16[512,128]{1,0:T(8,128)(2,1)} %bitcast.18, bf16[512,128]{1,0:T(8,128)(2,1)} %bitcast.21, bf16[4096,128]{1,0:T(8,128)(2,1)} %bitcast.19, ...), custom_call_target="tpu_custom_call" | custom-call | tf_op jit(solution)/shard_map/pallas_call | solution.py:485
  34.6 0.0 copy-start
  34.6 0.0 copy-start.1
  34.7 57.2 %shard_map.111 = (bf16[4096,128]{1,0:T(8,128)(2,1)}, bf16[10,512,256]{2,1,0:T(8,128)(2,1)}, f32[8,128]{1,0:T(8,128)}, s32[40]{0:T(128)}) custom-call(s32[8]{0:T(128)} %bitcast.27, bf16[32,512,128]{2,1,0:T(8,128)(2,1)} %get-tuple-element.16.kn_hbm, bf16[32,512,128]{2,1,0:T(8,128)(2,1)} %get-tuple-element.17.v_hbm, ...), custom_call_target="tpu_custom_call" | custom-call | tf_op jit(solution)/shard_map/pallas_call | solution.py:504
  91.8 37.3 %shard_map.112 = (f32[512,128]{1,0:T(8,128)}, bf16[512,128]{1,0:T(8,128)(2,1)}, f32[8,128]{1,0:T(8,128)}) custom-call(s32[40]{0:T(128)} %get-tuple-element.21.slot_ref, bf16[10,512,256]{2,1,0:T(8,128)(2,1)} %get-tuple-element.22.tile_hbm, f32[8,128]{1,0:T(8,128)} %get-tuple-element.23.g_ref), custom_call_target="tpu_custom_call" | custom-call | tf_op jit(solution)/shard_map/pallas_call | solution.py:345
  129.1 1.3 slice_bitcast_fusion
  130.4 0.0 copy-done
  130.4 0.0 copy-done.1
  130.4 1.2 fusion
  131.6 1.8 %fusion.7 = bf16[512,1,128]{2,0,1:T(8,128)(2,1)} fusion(f32[512,128]{1,0:T(8,128)} %get-tuple-element.24, f32[512]{0:T(512)S(1)} %get-tuple-element.32, f32[128]{0:T(128)S(1)} %copy-done.1, f32[512]{0:T(512)S(1)} %get-tuple-element.31, bf16[512,1,128]{2,0,1:T(8,128)(2,1)S(1)} %copy-done), kind=kLoop, calls=%fused_computation.10 | loop fusion | flops 524288 | bytes 528896 | tf_op jit(solution)/shard_map/reshape | solution.py:544
  133.4 1.6 %copy.13 = bf16[512,1,128]{2,0,1:T(8,128)(2,1)} copy(bf16[512,1,128]{2,0,1:T(8,128)(2,1)} %bitcast.22) | data formatting | bytes 262144
  (1 shorter events, 0.0 us)
Async XLA Ops:
  34.6 95.7 %copy-start = (bf16[512,1,128]{2,0,1:T(8,128)(2,1)S(1)}, bf16[512,1,128]{2,0,1:T(8,128)(2,1)}, u32[]{:S(2)}) copy-start(bf16[512,1,128]{2,0,1:T(8,128)(2,1)} %param.8) | copy-start | bytes 393220
  34.6 95.7 %copy-start.1 = (f32[128]{0:T(128)S(1)}, f32[128]{0:T(128)}, u32[]{:S(2)}) copy-start(f32[128]{0:T(128)} %param.12) | copy-start | bytes 1540

commit v6 on v5

--- a/solution.py
+++ b/solution.py
@@ -191,11 +191,13 @@
     return (z * 8 + x * 2 + c, y)
 
 
-def greet(devices):
-    barrier = pltpu.get_barrier_semaphore()
+def hail(devices):
     for d in devices:
-        pl.semaphore_signal(barrier, inc=1, device_id=d, device_id_type=MESH)
-    pl.semaphore_wait(barrier, len(devices))
+        pl.semaphore_signal(pltpu.get_barrier_semaphore(), inc=1, device_id=d, device_id_type=MESH)
+
+
+def settle(devices):
+    pl.semaphore_wait(pltpu.get_barrier_semaphore(), len(devices))
 
 
 def scatter_kernel(slot_ref, tile_hbm, g_ref, dk_ref, dv_ref, gout_ref,
@@ -210,10 +212,11 @@
             return peer(z, (x + off) % 4, c, y)
         return peer(z, x, c, (y + off) % 4)
 
-    fetch = pltpu.make_async_copy(tile_hbm, tile_ref, tsem)
+    fetch = pltpu.make_async_copy(tile_hbm.at[0:10], tile_ref, tsem)
     fetch.start()
     sib = peer(z, x, 1 - c, y)
-    greet([sib] + [along(a, o) for a in "zxy" for o in (1, 2, 3)])
+    friends = [sib] + [along(a, o) for a in "zxy" for o in (1, 2, 3)]
+    hail(friends)
     pending = []
 
     def send(src, dst, ss, rs, to):
@@ -223,9 +226,6 @@
         pending.append(cp)
         return cp
 
-    fetch.wait()
-    gcp = send(g_ref, GS, sg.at[0], rg.at[0], sib)
-
     axes = (("z", "x"), ("x", "z"))
     coord = {"z": z, "x": x}
 
@@ -236,13 +236,23 @@
         return slice(half * 128, half * 128 + 128)
 
     first = {}
+
+    def fill(half, off):
+        u = (coord[axes[half][0]] + off) % 4
+
+        @pl.loop(0, 4)
+        def _(w):
+            A[half, off, w] = tile_ref[slot_ref[block(half, u, w, 1 - c)], :, cols(half)]
+
+    fetch.wait()
+    fill(0, 2)
+    fill(1, 2)
+    settle(friends)
+    gcp = send(g_ref, GS, sg.at[0], rg.at[0], sib)
     for off in (2, 1, 3, 0):
         for half in (0, 1):
-            u = (coord[axes[half][0]] + off) % 4
-
-            @pl.loop(0, 4)
-            def _(w):
-                A[half, off, w] = tile_ref[slot_ref[block(half, u, w, 1 - c)], :, cols(half)]
+            if off != 2:
+                fill(half, off)
             first[half, off] = send(A.at[half, off], B.at[half, off], s0.at[half * 4 + off], r0.at[half * 4 + off], sib)
 
     def group(G, base, kind):
@@ -356,21 +366,26 @@
             pltpu.VMEM((8, 128), F32), pltpu.VMEM((4, 8, 128), F32), pltpu.VMEM((4, 8, 128), F32), pltpu.VMEM((4, 8, 128), F32),
             D((8,)), D((8,)), D((2, 6)), D((2, 6)), D((2, 6)), D((2, 6)), D((10,)), D((10,)),
         ],
-        compiler_params=pltpu.CompilerParams(collective_id=1, has_side_effects=True, vmem_limit_bytes=62 * 2 ** 20),
+        compiler_params=pltpu.CompilerParams(collective_id=1, has_side_effects=True, vmem_limit_bytes=52 * 2 ** 20),
     )(slot, tile, g)
 
 
-def gather_kernel(k_ref, v_ref, q_ref, do_ref, qg_ref, kg_ref, ko_ref, vo_ref, rows_out, cols_out,
-                  kn_ref, q32, do32, rows, cols, lsem, psem, ss, rs):
+def gather_kernel(k_ref, v_ref, q_hbm, do_hbm, qg_ref, kg_ref, ko_ref, vo_ref, rows_out, cols_out,
+                  kn_ref, qb, db, q32, do32, isem, rows, cols, lsem, psem, ss, rs):
     z, x, c, y = place()
 
     def along(axis, off):
         return peer((z + off) % 4, x, c, y) if axis == "z" else peer(z, (x + off) % 4, c, y)
 
+    sib = peer(z, x, 1 - c, y)
+    friends = [sib] + [along(a, o) for a in "zx" for o in (1, 3)]
+    hail(friends)
+    loads = [pltpu.make_async_copy(q_hbm, qb, isem.at[0]), pltpu.make_async_copy(do_hbm, db, isem.at[1])]
+    for cp in loads:
+        cp.start()
     _, _, kn = norm_fwd(k_ref[...], kg_ref[...])
     kn_ref[...] = kn
-    sib = peer(z, x, 1 - c, y)
-    greet([sib] + [along(a, o) for a in "zx" for o in (1, 3)])
+    settle(friends)
     coord = {"z": z, "x": x}
     pending = []
     sibling = []
@@ -406,9 +421,6 @@
     for half, (src, out, u, w) in enumerate(halves):
         got[half, "u+"] = send(half, 0, 0, full, along(u, 1), src)
         got[half, "u-"] = send(half, 0, 0, full, along(u, 3), src)
-    q32[...] = q_ref[...].astype(F32)
-    do32[...] = do_ref[...].astype(F32)
-
     def prep(h):
         x = q32[pl.ds(h, 512, stride=8), :]
         _, _, qn = norm_fwd(x, qg_ref[...])
@@ -427,6 +439,10 @@
         got[half, 0, "w+"] = send(half, 0, 0, full, along(w, 1), src)
         got[half, 0, "w-"] = send(half, 0, 0, full, along(w, 3), src)
         sibling.append(send(half, 0, 0, full, sib, src))
+    for cp in loads:
+        cp.wait()
+    q32[...] = qb[...].astype(F32)
+    do32[...] = db[...].astype(F32)
     prep(0)
     for half, (src, out, u, w) in enumerate(halves):
         got[half, "u+"].wait_recv()
@@ -486,10 +502,11 @@
         gather_kernel,
         out_shape=(jax.ShapeDtypeStruct((32, 512, 128), BF), jax.ShapeDtypeStruct((32, 512, 128), BF),
                    jax.ShapeDtypeStruct((8, 3, 512, 128), BF), jax.ShapeDtypeStruct((8, 2, 128, 512), BF)),
-        in_specs=[vm] * 6,
+        in_specs=[vm, vm, anys, anys, vm, vm],
         out_specs=(anys,) * 4,
         scratch_shapes=[
-            pltpu.VMEM((512, 128), BF), pltpu.VMEM((4096, 128), F32), pltpu.VMEM((4096, 128), F32),
+            pltpu.VMEM((512, 128), BF), pltpu.VMEM((4096, 128), BF), pltpu.VMEM((4096, 128), BF),
+            pltpu.VMEM((4096, 128), F32), pltpu.VMEM((4096, 128), F32), D((2,)),
             pltpu.VMEM((8, 3, 512, 128), BF), pltpu.VMEM((8, 2, 128, 512), BF),
             D((2,)), D((2, 8)), D((2, 36)), D((2, 36)),
         ],
@@ -505,7 +522,7 @@
         attn_kernel,
         out_shape=(
             jax.ShapeDtypeStruct((512 * H, 128), BF),
-            jax.ShapeDtypeStruct((10, 512, 256), BF),
+            jax.ShapeDtypeStruct((64, 512, 256), BF),
             jax.ShapeDtypeStruct((8, 128), F32),
             jax.ShapeDtypeStruct((40,), jnp.int32),
         ),

time: 135 us -> 131 us (0.970)
  Pallas kernels: 128 us -> 126 us
  other arithmetic: 2.98 us -> 1.09 us
where the time goes in v6:
time: 131 us
  Pallas kernels  126 us (96%)
  local copies, waits for them, and re-layouts  2.52 us (2%)
    pallas_call x1, Pallas kernels, attn(): pl.pallas_call(attn_kernel, out_shape=(jax.ShapeDtypeStruct((512 * H, 128...  57.1 us
    pallas_call x1, Pallas kernels, scatter(): pl.pallas_call(scatter_kernel, out_shape=(jax.ShapeDtypeStruct((512, 128)...  36.1 us
    pallas_call x1, Pallas kernels, gather(): pl.pallas_call(gather_kernel, out_shape=(jax.ShapeDtypeStruct((32, 512, 1...  33.2 us

profile of v6, /device:TPU:0, one launch (start us, length us, event | category | flops | bytes accessed | tf_op | source)
XLA Modules:
  0.0 130.6 jit_solution(4989337153269160395)
XLA Ops:
  0.6 33.2 %shard_map.110 = (bf16[32,512,128]{2,1,0:T(8,128)(2,1)}, bf16[32,512,128]{2,1,0:T(8,128)(2,1)}, bf16[8,3,512,128]{3,2,1,0:T(8,128)(2,1)}, bf16[8,2,128,512]{3,2,1,0:T(8,128)(2,1)}) custom-call(bf16[512,128]{1,0:T(8,128)(2,1)} %bitcast.19, bf16[512,128]{1,0:T(8,128)(2,1)} %bitcast.22, bf16[4096,128]{1,0:T(8,128)(2,1)} %bitcast.20, ...), custom_call_target="tpu_custom_call" | custom-call | tf_op jit(solution)/shard_map/pallas_call | solution.py:501
  33.8 57.1 %shard_map.111 = (bf16[4096,128]{1,0:T(8,128)(2,1)}, bf16[64,512,256]{2,1,0:T(8,128)(2,1)}, f32[8,128]{1,0:T(8,128)}, s32[40]{0:T(128)}) custom-call(s32[8]{0:T(128)} %bitcast.27, bf16[32,512,128]{2,1,0:T(8,128)(2,1)} %get-tuple-element.16.kn_hbm, bf16[32,512,128]{2,1,0:T(8,128)(2,1)} %get-tuple-element.17.v_hbm, ...), custom_call_target="tpu_custom_call" | custom-call | tf_op jit(solution)/shard_map/pallas_call | solution.py:521
  90.9 0.0 copy-start
  90.9 0.7 copy-done
  91.6 0.0 copy-start.1
  91.6 0.7 copy-done.1
  92.2 0.0 copy-start.2
  92.2 0.0 copy-start.3
  92.2 36.1 %shard_map.112 = (f32[512,128]{1,0:T(8,128)S(1)}, bf16[512,128]{1,0:T(8,128)(2,1)S(1)}, f32[8,128]{1,0:T(8,128)S(1)}) custom-call(s32[40]{0:T(128)S(1)} %copy-done.1, bf16[64,512,256]{2,1,0:T(8,128)(2,1)} %get-tuple-element.22.tile_hbm, f32[8,128]{1,0:T(8,128)S(1)} %copy-done), custom_call_target="tpu_custom_call" | custom-call | tf_op jit(solution)/shard_map/pallas_call | solution.py:355
  128.4 0.5 slice_bitcast_fusion
  128.9 0.0 copy-done.2
  128.9 0.0 copy-done.3
  128.9 0.2 fusion
  129.1 0.9 fusion.7
  130.0 0.7 copy.13
  (1 shorter events, 0.0 us)
Async XLA Ops:
  90.9 0.7 copy-start
  91.6 0.7 copy-start.1
  92.2 36.7 %copy-start.2 = (bf16[512,1,128]{2,0,1:T(8,128)(2,1)S(1)}, bf16[512,1,128]{2,0,1:T(8,128)(2,1)}, u32[]{:S(2)}) copy-start(bf16[512,1,128]{2,0,1:T(8,128)(2,1)} %param.8) | copy-start | bytes 393220
  92.2 36.7 %copy-start.3 = (f32[128]{0:T(128)S(1)}, f32[128]{0:T(128)}, u32[]{:S(2)}) copy-start(f32[128]{0:T(128)} %param.12) | copy-start | bytes 1540

commit v7 on v6

--- a/solution.py
+++ b/solution.py
@@ -35,7 +35,7 @@
     return op(x.reshape(x.shape[0] // 8, 8, x.shape[1]), axis=0)
 
 def attn_kernel(idx_ref, kn_hbm, v_hbm, rows_hbm, cols_hbm, qgain_ref, kgain_ref,
-                dq_ref, tile_hbm, g_ref, slot_ref, tile_ref, rows_ref, cols_ref, kg_ref, gq_ref,
+                dq_ref, tile_hbm, g_hbm, slot_ref, tile_ref, g_ref, rows_ref, cols_ref, kg_ref, gq_ref,
                 kb, vb, kT, S, DP, E, dk, dv, dqT, mrow, drow, qs, dos, dq32, sem, hsem):
     H = rows_hbm.shape[0]
     J = 9
@@ -175,6 +175,9 @@
     part_k = jnp.sum(kg_ref[...], axis=0, keepdims=True) / kgain_ref[...]
     row = lax.broadcasted_iota(jnp.int32, (8, 128), 0)
     g_ref[...] = jnp.where(row == 0, part_q, jnp.where(row == 1, part_k, 0.0))
+    gcp = pltpu.make_async_copy(g_ref, g_hbm.at[0:8], sem.at[0, J])
+    gcp.start()
+    gcp.wait()
     for j in range(J + 1):
         tile_out(j).wait()
 
@@ -200,8 +203,8 @@
     pl.semaphore_wait(pltpu.get_barrier_semaphore(), len(devices))
 
 
-def scatter_kernel(slot_ref, tile_hbm, g_ref, dk_ref, dv_ref, gout_ref,
-                   tile_ref, tsem, A, B, cur, R1, R2, T, Q1, Q2, GS, GZ, GX, GY,
+def scatter_kernel(slot_ref, tile_hbm, g_hbm, dk_ref, dv_ref, gout_ref,
+                   tile_ref, g_ref, tsem, A, B, cur, R1, R2, T, Q1, Q2, GS, GZ, GX, GY,
                    s0, r0, s1, r1, s2, r2, sg, rg):
     z, x, c, y = place()
 
@@ -212,8 +215,10 @@
             return peer(z, (x + off) % 4, c, y)
         return peer(z, x, c, (y + off) % 4)
 
-    fetch = pltpu.make_async_copy(tile_hbm.at[0:10], tile_ref, tsem)
+    fetch = pltpu.make_async_copy(tile_hbm.at[0:10], tile_ref, tsem.at[0])
     fetch.start()
+    gfetch = pltpu.make_async_copy(g_hbm.at[0:8], g_ref, tsem.at[1])
+    gfetch.start()
     sib = peer(z, x, 1 - c, y)
     friends = [sib] + [along(a, o) for a in "zxy" for o in (1, 2, 3)]
     hail(friends)
@@ -239,14 +244,16 @@
 
     def fill(half, off):
         u = (coord[axes[half][0]] + off) % 4
+        cw = coord[axes[half][1]]
 
         @pl.loop(0, 4)
-        def _(w):
-            A[half, off, w] = tile_ref[slot_ref[block(half, u, w, 1 - c)], :, cols(half)]
+        def _(p):
+            A[half, off, p] = tile_ref[slot_ref[block(half, u, (cw + p + 2) % 4, 1 - c)], :, cols(half)]
 
     fetch.wait()
     fill(0, 2)
     fill(1, 2)
+    gfetch.wait()
     settle(friends)
     gcp = send(g_ref, GS, sg.at[0], rg.at[0], sib)
     for off in (2, 1, 3, 0):
@@ -269,10 +276,12 @@
         first[half, off].wait_recv()
         u = (coord[axes[half][0]] + off) % 4
 
+        cw = coord[axes[half][1]]
+
         @pl.loop(0, 4)
-        def _(w):
-            mine = tile_ref[slot_ref[block(half, u, w, c)], :, cols(half)]
-            cur[half, off, w] = (mine.astype(F32) + B[half, off, w].astype(F32)).astype(BF)
+        def _(p):
+            mine = tile_ref[slot_ref[block(half, u, (cw + p + 2) % 4, c)], :, cols(half)]
+            cur[half, off, p] = (mine.astype(F32) + B[half, off, p].astype(F32)).astype(BF)
 
     def s1send(k, half, src, dst, off):
         return send(src, dst, s1.at[half, k], r1.at[half, k], along(axes[half][0], off))
@@ -292,19 +301,19 @@
     gz = group(GZ, 0, "z")
     for half in (0, 1):
         own_sum(half, 0)
+    def merge(half, k, p):
+        off = 1 if k == 0 else 3
+        cur[half, off, p] = (cur[half, off, p].astype(F32) + R1[half, k, p % 2].astype(F32)).astype(BF)
+        c1[half, 4 + p] = s1send(4 + p, half, cur.at[half, off, p], R2.at[half, k, p], off)
+
     for half in (0, 1):
         c1[half, 0].wait_recv()
-
-        @pl.loop(0, 2)
-        def _(w):
-            cur[half, 1, w] = (cur[half, 1, w].astype(F32) + R1[half, 0, w].astype(F32)).astype(BF)
-        c1[half, 4] = s1send(4, half, cur.at[half, 1, 0:2], R2.at[half, 0, 0:2], 1)
+        merge(half, 0, 0)
         c1[half, 1].wait_recv()
-
-        @pl.loop(0, 2)
-        def _(w):
-            cur[half, 3, w + 2] = (cur[half, 3, w + 2].astype(F32) + R1[half, 1, w].astype(F32)).astype(BF)
-        c1[half, 5] = s1send(5, half, cur.at[half, 3, 2:4], R2.at[half, 1, 2:4], 3)
+        merge(half, 1, 3)
+    for half in (0, 1):
+        merge(half, 0, 1)
+        merge(half, 1, 2)
     GX[x] = gsum(GZ, gz)
     gx = group(GX, 3, "x")
 
@@ -313,20 +322,24 @@
 
     lo, hi = slice(0, 256), slice(256, 512)
     c2 = {}
-    for half in (0, 1):
-        for k in (2, 3, 4, 5):
-            c1[half, k].wait_recv()
-        cw = coord[axes[half][1]]
-
-        @pl.loop(0, 4)
-        def _(o):
-            w = (cw + o) % 4
-            T[half, o] = (cur[half, 0, w].astype(F32) + R2[half, 0, w].astype(F32)
-                          + R2[half, 1, w].astype(F32)).astype(BF)
+
+    def total(half, p):
+        c1[half, 4 + p].wait_recv()
+        T[half, (p + 2) % 4] = (cur[half, 0, p].astype(F32) + R2[half, 0, p].astype(F32)
+                                + R2[half, 1, p].astype(F32)).astype(BF)
+
+    for half in (0, 1):
+        c1[half, 2].wait_recv()
+        c1[half, 3].wait_recv()
+        total(half, 0)
         c2[half, 0] = s2send(0, half, T.at[half, 2, lo], Q1.at[half, 0], 1)
         c2[half, 1] = s2send(1, half, T.at[half, 2, hi], Q1.at[half, 1], 3)
+        total(half, 3)
         c2[half, 2] = s2send(2, half, T.at[half, 1, hi], Q2.at[half, 0, hi], 1)
+    for half in (0, 1):
+        total(half, 1)
         c2[half, 3] = s2send(3, half, T.at[half, 3, lo], Q2.at[half, 1, lo], 3)
+        total(half, 2)
     GY[y] = gsum(GX, gx)
     gy = group(GY, 6, "y")
     for half in (0, 1):
@@ -356,15 +369,15 @@
         scatter_kernel,
         out_shape=(jax.ShapeDtypeStruct((512, 128), F32), jax.ShapeDtypeStruct((512, 128), BF),
                    jax.ShapeDtypeStruct((8, 128), F32)),
-        in_specs=[pl.BlockSpec(memory_space=pltpu.SMEM), pl.BlockSpec(memory_space=pl.ANY), V()],
+        in_specs=[pl.BlockSpec(memory_space=pltpu.SMEM), pl.BlockSpec(memory_space=pl.ANY), pl.BlockSpec(memory_space=pl.ANY)],
         out_specs=(V(), V(), V()),
         scratch_shapes=[
-            pltpu.VMEM((10, 512, 256), BF), D(()),
+            pltpu.VMEM((10, 512, 256), BF), pltpu.VMEM((8, 128), F32), D((2,)),
             pltpu.VMEM((2, 4, 4, 512, 128), BF), pltpu.VMEM((2, 4, 4, 512, 128), BF), pltpu.VMEM((2, 4, 4, 512, 128), BF),
             pltpu.VMEM((2, 2, 2, 512, 128), BF), pltpu.VMEM((2, 2, 4, 512, 128), BF),
             pltpu.VMEM((2, 4, 512, 128), BF), pltpu.VMEM((2, 2, 256, 128), BF), pltpu.VMEM((2, 2, 512, 128), BF),
             pltpu.VMEM((8, 128), F32), pltpu.VMEM((4, 8, 128), F32), pltpu.VMEM((4, 8, 128), F32), pltpu.VMEM((4, 8, 128), F32),
-            D((8,)), D((8,)), D((2, 6)), D((2, 6)), D((2, 6)), D((2, 6)), D((10,)), D((10,)),
+            D((8,)), D((8,)), D((2, 8)), D((2, 8)), D((2, 6)), D((2, 6)), D((10,)), D((10,)),
         ],
         compiler_params=pltpu.CompilerParams(collective_id=1, has_side_effects=True, vmem_limit_bytes=52 * 2 ** 20),
     )(slot, tile, g)
@@ -523,13 +536,13 @@
         out_shape=(
             jax.ShapeDtypeStruct((512 * H, 128), BF),
             jax.ShapeDtypeStruct((64, 512, 256), BF),
-            jax.ShapeDtypeStruct((8, 128), F32),
+            jax.ShapeDtypeStruct((32768, 128), F32),
             jax.ShapeDtypeStruct((40,), jnp.int32),
         ),
         in_specs=[pl.BlockSpec(memory_space=pltpu.SMEM), A(), A(), A(), A(), V(), V()],
-        out_specs=(V(), A(), V(), pl.BlockSpec(memory_space=pltpu.SMEM)),
+        out_specs=(V(), A(), A(), pl.BlockSpec(memory_space=pltpu.SMEM)),
         scratch_shapes=[
-            pltpu.VMEM((10, 512, 256), BF),
+            pltpu.VMEM((10, 512, 256), BF), pltpu.VMEM((8, 128), F32),
             pltpu.VMEM((H, 3, 512, 128), BF), pltpu.VMEM((H, 2, 128, 512), BF),
             pltpu.VMEM((8, 128), F32), pltpu.VMEM((8, 128), F32),
             pltpu.VMEM((9, 512, 128), BF), pltpu.VMEM((9, 512, 128), BF),

time: 131 us -> 128 us (0.977)
  Pallas kernels: 126 us -> 124 us
    pallas_call x1, Pallas kernels: 36.1 us -> 33.6 us  [scatter(): pl.pallas_call(scatter_kernel, out_shape=(jax.ShapeDtypeStruct((512, 128)...]
where the time goes in v7:
time: 128 us
  Pallas kernels  124 us (97%)
  local copies, waits for them, and re-layouts  1.83 us (1%)
    pallas_call x1, Pallas kernels, attn(): pl.pallas_call(attn_kernel, out_shape=(jax.ShapeDtypeStruct((512 * H, 128...  57.5 us
    pallas_call x1, Pallas kernels, scatter(): pl.pallas_call(scatter_kernel, out_shape=(jax.ShapeDtypeStruct((512, 128)...  33.6 us
    pallas_call x1, Pallas kernels, gather(): pl.pallas_call(gather_kernel, out_shape=(jax.ShapeDtypeStruct((32, 512, 1...  33.2 us

profile of v7, /device:TPU:0, one launch (start us, length us, event | category | flops | bytes accessed | tf_op | source)
XLA Modules:
  0.0 127.8 jit_solution(17187934267589674516)
XLA Ops:
  0.6 33.2 %shard_map.110 = (bf16[32,512,128]{2,1,0:T(8,128)(2,1)}, bf16[32,512,128]{2,1,0:T(8,128)(2,1)}, bf16[8,3,512,128]{3,2,1,0:T(8,128)(2,1)}, bf16[8,2,128,512]{3,2,1,0:T(8,128)(2,1)}) custom-call(bf16[512,128]{1,0:T(8,128)(2,1)} %bitcast.19, bf16[512,128]{1,0:T(8,128)(2,1)} %bitcast.22, bf16[4096,128]{1,0:T(8,128)(2,1)} %bitcast.20, ...), custom_call_target="tpu_custom_call" | custom-call | tf_op jit(solution)/shard_map/pallas_call | solution.py:514
  33.8 57.5 %shard_map.111 = (bf16[4096,128]{1,0:T(8,128)(2,1)}, bf16[64,512,256]{2,1,0:T(8,128)(2,1)}, f32[32768,128]{1,0:T(8,128)}, s32[40]{0:T(128)}) custom-call(s32[8]{0:T(128)} %bitcast.27, bf16[32,512,128]{2,1,0:T(8,128)(2,1)} %get-tuple-element.16.kn_hbm, bf16[32,512,128]{2,1,0:T(8,128)(2,1)} %get-tuple-element.17.v_hbm, ...), custom_call_target="tpu_custom_call" | custom-call | tf_op jit(solution)/shard_map/pallas_call | solution.py:534
  91.3 0.0 copy-start
  91.3 0.6 copy-done
  91.9 0.0 copy-start.1
  91.9 0.0 copy-start.2
  91.9 33.6 %shard_map.112 = (f32[512,128]{1,0:T(8,128)S(1)}, bf16[512,128]{1,0:T(8,128)(2,1)S(1)}, f32[8,128]{1,0:T(8,128)S(1)}) custom-call(s32[40]{0:T(128)S(1)} %copy-done, bf16[64,512,256]{2,1,0:T(8,128)(2,1)} %get-tuple-element.22.tile_hbm, f32[32768,128]{1,0:T(8,128)} %get-tuple-element.23.g_hbm), custom_call_target="tpu_custom_call" | custom-call | tf_op jit(solution)/shard_map/pallas_call | solution.py:368
  125.5 0.5 slice_bitcast_fusion
  126.0 0.0 copy-done.1
  126.0 0.0 copy-done.2
  126.0 0.2 fusion
  126.3 0.9 fusion.7
  127.1 0.7 copy.13
  (1 shorter events, 0.0 us)
Async XLA Ops:
  91.3 0.7 copy-start
  91.9 34.1 %copy-start.1 = (bf16[512,1,128]{2,0,1:T(8,128)(2,1)S(1)}, bf16[512,1,128]{2,0,1:T(8,128)(2,1)}, u32[]{:S(2)}) copy-start(bf16[512,1,128]{2,0,1:T(8,128)(2,1)} %param.8) | copy-start | bytes 393220
  91.9 34.1 %copy-start.2 = (f32[128]{0:T(128)S(1)}, f32[128]{0:T(128)}, u32[]{:S(2)}) copy-start(f32[128]{0:T(128)} %param.12) | copy-start | bytes 1540

commit v8 on v7

--- a/solution.py
+++ b/solution.py
@@ -35,7 +35,7 @@
     return op(x.reshape(x.shape[0] // 8, 8, x.shape[1]), axis=0)
 
 def attn_kernel(idx_ref, kn_hbm, v_hbm, rows_hbm, cols_hbm, qgain_ref, kgain_ref,
-                dq_ref, tile_hbm, g_hbm, slot_ref, tile_ref, g_ref, rows_ref, cols_ref, kg_ref, gq_ref,
+                dq_hbm, tile_hbm, g_hbm, slot_ref, dq_ref, tile_ref, g_ref, rows_ref, cols_ref, kg_ref, gq_ref,
                 kb, vb, kT, S, DP, E, dk, dv, dqT, mrow, drow, qs, dos, dq32, sem, hsem):
     H = rows_hbm.shape[0]
     J = 9
@@ -170,16 +170,26 @@
     step(H, False, True, True)
     step(H + 1, False, False, True)
 
-    dq_ref[...] = dq32[...].astype(BF)
     part_q = jnp.sum(gq_ref[...], axis=0, keepdims=True)
     part_k = jnp.sum(kg_ref[...], axis=0, keepdims=True) / kgain_ref[...]
     row = lax.broadcasted_iota(jnp.int32, (8, 128), 0)
     g_ref[...] = jnp.where(row == 0, part_q, jnp.where(row == 1, part_k, 0.0))
     gcp = pltpu.make_async_copy(g_ref, g_hbm.at[0:8], sem.at[0, J])
     gcp.start()
+
+    def dq_out(b):
+        rows = pl.ds(b * 1024, 1024)
+        return pltpu.make_async_copy(dq_ref.at[rows], dq_hbm.at[rows], hsem.at[0, b])
+
+    for b in range(4):
+        rows = pl.ds(b * 1024, 1024)
+        dq_ref[rows] = dq32[rows].astype(BF)
+        dq_out(b).start()
     gcp.wait()
     for j in range(J + 1):
         tile_out(j).wait()
+    for b in range(4):
+        dq_out(b).wait()
 
 
 MESH = pl.DeviceIdType.MESH
@@ -540,9 +550,9 @@
             jax.ShapeDtypeStruct((40,), jnp.int32),
         ),
         in_specs=[pl.BlockSpec(memory_space=pltpu.SMEM), A(), A(), A(), A(), V(), V()],
-        out_specs=(V(), A(), A(), pl.BlockSpec(memory_space=pltpu.SMEM)),
+        out_specs=(A(), A(), A(), pl.BlockSpec(memory_space=pltpu.SMEM)),
         scratch_shapes=[
-            pltpu.VMEM((10, 512, 256), BF), pltpu.VMEM((8, 128), F32),
+            pltpu.VMEM((512 * H, 128), BF), pltpu.VMEM((10, 512, 256), BF), pltpu.VMEM((8, 128), F32),
             pltpu.VMEM((H, 3, 512, 128), BF), pltpu.VMEM((H, 2, 128, 512), BF),
             pltpu.VMEM((8, 128), F32), pltpu.VMEM((8, 128), F32),
             pltpu.VMEM((9, 512, 128), BF), pltpu.VMEM((9, 512, 128), BF),

time: 128 us -> 128 us (level)
  no operation moved by 1% of the time
where the time goes in v8:
time: 128 us
  Pallas kernels  124 us (97%)
  local copies, waits for them, and re-layouts  1.83 us (1%)
    pallas_call x1, Pallas kernels, attn(): pl.pallas_call(attn_kernel, out_shape=(jax.ShapeDtypeStruct((512 * H, 128...  57.3 us
    pallas_call x1, Pallas kernels, scatter(): pl.pallas_call(scatter_kernel, out_shape=(jax.ShapeDtypeStruct((512, 128)...  33.5 us
    pallas_call x1, Pallas kernels, gather(): pl.pallas_call(gather_kernel, out_shape=(jax.ShapeDtypeStruct((32, 512, 1...  33.2 us

profile of v8, /device:TPU:0, one launch (start us, length us, event | category | flops | bytes accessed | tf_op | source)
XLA Modules:
  0.0 127.6 jit_solution(6369249899566723809)
XLA Ops:
  0.6 33.2 %shard_map.110 = (bf16[32,512,128]{2,1,0:T(8,128)(2,1)}, bf16[32,512,128]{2,1,0:T(8,128)(2,1)}, bf16[8,3,512,128]{3,2,1,0:T(8,128)(2,1)}, bf16[8,2,128,512]{3,2,1,0:T(8,128)(2,1)}) custom-call(bf16[512,128]{1,0:T(8,128)(2,1)} %bitcast.19, bf16[512,128]{1,0:T(8,128)(2,1)} %bitcast.22, bf16[4096,128]{1,0:T(8,128)(2,1)} %bitcast.20, ...), custom_call_target="tpu_custom_call" | custom-call | tf_op jit(solution)/shard_map/pallas_call | solution.py:524
  33.8 57.3 %shard_map.111 = (bf16[4096,128]{1,0:T(8,128)(2,1)}, bf16[64,512,256]{2,1,0:T(8,128)(2,1)}, f32[32768,128]{1,0:T(8,128)}, s32[40]{0:T(128)}) custom-call(s32[8]{0:T(128)} %bitcast.27, bf16[32,512,128]{2,1,0:T(8,128)(2,1)} %get-tuple-element.16.kn_hbm, bf16[32,512,128]{2,1,0:T(8,128)(2,1)} %get-tuple-element.17.v_hbm, ...), custom_call_target="tpu_custom_call" | custom-call | tf_op jit(solution)/shard_map/pallas_call | solution.py:544
  91.1 0.0 copy-start
  91.1 0.6 copy-done
  91.8 0.0 copy-start.1
  91.8 0.0 copy-start.2
  91.8 33.5 %shard_map.112 = (f32[512,128]{1,0:T(8,128)S(1)}, bf16[512,128]{1,0:T(8,128)(2,1)S(1)}, f32[8,128]{1,0:T(8,128)S(1)}) custom-call(s32[40]{0:T(128)S(1)} %copy-done, bf16[64,512,256]{2,1,0:T(8,128)(2,1)} %get-tuple-element.22.tile_hbm, f32[32768,128]{1,0:T(8,128)} %get-tuple-element.23.g_hbm), custom_call_target="tpu_custom_call" | custom-call | tf_op jit(solution)/shard_map/pallas_call | solution.py:378
  125.3 0.5 slice_bitcast_fusion
  125.8 0.0 copy-done.1
  125.8 0.0 copy-done.2
  125.8 0.2 fusion
  126.1 0.9 fusion.7
  126.9 0.7 copy.13
  (1 shorter events, 0.0 us)
Async XLA Ops:
  91.1 0.7 copy-start
  91.8 34.1 %copy-start.1 = (bf16[512,1,128]{2,0,1:T(8,128)(2,1)S(1)}, bf16[512,1,128]{2,0,1:T(8,128)(2,1)}, u32[]{:S(2)}) copy-start(bf16[512,1,128]{2,0,1:T(8,128)(2,1)} %param.8) | copy-start | bytes 393220
  91.8 34.1 %copy-start.2 = (f32[128]{0:T(128)S(1)}, f32[128]{0:T(128)}, u32[]{:S(2)}) copy-start(f32[128]{0:T(128)} %param.12) | copy-start | bytes 1540
